TPU v7x, 32 devices: a whole 2x2x4 slice. The times are simulated.
32 devices in a mesh: grp: 2 (over x), row: 8 (over z, y), col: 2 (over core).
Axes of the slice: x: 2, y: 2, z: 4, core: 2. Of those that a mesh axis runs over, the one named last changes fastest.
Arguments:
- a_tiles: bfloat16 [32768, 2048], P(('grp', 'row'), 'col'), parts along dimension 0, may hold values from -6 to 6
- b_tiles: bfloat16 [4096, 4096], P(('grp', 'row'), 'col'), parts along dimension 0, may hold values from -0.125 to 0.125
- a_mask: int32 [128, 8], P('grp'), parts along dimension 0, may hold values from 0 to 1, as said below
- b_mask: int32 [16, 16], P('grp'), parts along dimension 0, may hold values 0 or 1
- c_given: bfloat16 [32768, 4096], P(('grp', 'row'), 'col'), parts along dimension 0, may hold values from -6 to 6
Outputs:
- c_result: bfloat16 [32768, 4096], P(('grp', 'row'), 'col'), parts along dimension 0
There are 2 independent parts, one for each index of `grp`. A program takes and returns all parts, laid end to end along the dimension named above; each array names one. Nothing has to cross between parts.
Inputs may be any that keep to these rules, and one draw needn't show every extreme that they name: `a_mask`: 1 where tile (i, k) of a_tiles is kept, else 0; the share of ones differs between tile rows. `b_mask`: 1 where tile (k, j) of b_tiles is kept, else 0.
All inputs are finite; a program needn't handle non-finite values.
Results may differ from a plain program's by a relative error of at most 0.001.
Values may be sent and summed in bfloat16 or wider, within the bound.
No kernel may reach another device: no remote copies, remote signals or barrier semaphores. Data moves between devices by JAX's collectives and lax.ppermute only.
A program may use at most 192 MiB of HBM per device.

v0:
```python
import jax
import jax.numpy as jnp
from jax import lax
from jax.sharding import PartitionSpec as P

TW = 256
STEPS = 8


def expand(source, flags):
    row_count, col_count = source.shape
    tile_rows, tile_cols = flags.shape
    shaped = source.reshape(tile_rows, row_count // tile_rows, tile_cols, col_count // tile_cols)
    kept = shaped * flags[:, None, :, None].astype(source.dtype)
    return kept.reshape(row_count, col_count)


def on_device(a_tiles, b_tiles, a_mask, b_mask, c_given):
    row_index = lax.axis_index("row")
    col_index = lax.axis_index("col")
    row_count, a_width = a_tiles.shape
    b_height, c_width = b_tiles.shape
    tile_rows = row_count // TW
    row_flags = lax.dynamic_slice(a_mask, (row_index * tile_rows, 0), (tile_rows, STEPS))
    a_flags = lax.dynamic_slice(
        row_flags, (0, col_index * (a_width // TW)), (tile_rows, a_width // TW)
    )
    a_kept = expand(a_tiles, a_flags)
    b_flags = lax.dynamic_slice(
        b_mask, (row_index * b_height // TW, col_index * (c_width // TW)), (1, c_width // TW)
    )
    b_kept = expand(b_tiles, b_flags)
    a_whole = lax.all_gather(a_kept, "col", axis=1, tiled=True)
    totals = jnp.dot(
        a_whole,
        lax.all_gather(b_kept, "row", axis=0, tiled=True),
        preferred_element_type=jnp.float32,
    )
    return (c_given.astype(jnp.float32) + totals).astype(jnp.bfloat16)


def solution(mesh):
    return jax.shard_map(
        on_device,
        mesh=mesh,
        in_specs=(
            P(("grp", "row"), "col"),
            P(("grp", "row"), "col"),
            P("grp", None),
            P("grp", None),
            P(("grp", "row"), "col"),
        ),
        out_specs=P(("grp", "row"), "col"),
        check_vma=False,
    )
```

profile of v0, /device:TPU:0, one launch (start us, length us, event | category | flops | bytes accessed | tf_op | source)
XLA Modules:
  0.0 196.3 jit_solution(3068210200990225036)
XLA Ops:
  6.5 0.0 all-gather.3.cloned.1.call-start
  6.5 0.8 dynamic-slice_convert_fusion
  7.3 0.1 copy.6
  7.4 0.0 copy-start
  7.4 1.1 mul.40
  8.6 1.0 copy.7
  9.6 0.0 copy-done
  9.6 0.0 copy-start.1
  9.6 4.2 %mul.42 = bf16[2048,1024]{1,0:T(8,128)(2,1)} multiply(bf16[2048,1024]{1,0:T(8,128)(2,1)S(1)} %copy-done, bf16[2048,1024]{1,0:T(8,128)(2,1)S(1)} %bitcast.10) | non-fusion elementwise | flops 2097152 | bytes 12582912 | tf_op jit(solution)/shard_map/mul | solution.py:14
  13.9 0.0 all-gather.3.cloned.1.call-update
  13.9 0.0 all-gather.5.cloned.1.call-start
  14.0 0.8 convert_bitcast_fusion
  14.7 0.1 broadcast_bitcast_fusion
  14.8 0.0 copy-done.1
  14.8 1.0 broadcast_multiply_fusion
  15.9 0.0 all-gather.5.cloned.1.call-update
  15.9 20.7 %all-gather.3.cloned.1.call-done = bf16[2048,2048]{1,0:T(8,128)(2,1)} async-done(((bf16[2048,1024]{1,0:T(8,128)(2,1)}), bf16[2048,2048]{1,0:T(8,128)(2,1)}) %all-gather.3.cloned.1.call-update) | async-done | bytes 8388624 | tf_op jit(solution)/shard_map/all_gather | solution.py:33
  36.6 128.3 %all-gather.5.cloned.1.call-done = bf16[2048,2048]{1,0:T(8,128)(2,1)} async-done(((bf16[256,2048]{1,0:T(8,128)(2,1)}), bf16[2048,2048]{1,0:T(8,128)(2,1)}) %all-gather.5.cloned.1.call-update) | async-done | bytes 8388624 | tf_op jit(solution)/shard_map/all_gather | solution.py:36
  164.9 24.6 %add_convert_fusion = bf16[2048,2048]{1,0:T(8,128)(2,1)} fusion(bf16[2048,2048]{1,0:T(8,128)(2,1)} %param.9, bf16[2048,2048]{1,0:T(8,128)(2,1)} %all-gather.3.cloned.1.call-done, bf16[2048,2048]{1,0:T(8,128)(2,1)} %all-gather.5.cloned.1.call-done), kind=kOutput, calls=%fused_computation | convolution fusion | flops 17192452096 | bytes 33554432 | tf_op jit(solution)/shard_map/dot_general | solution.py:34
  (1 shorter events, 0.0 us)
Async XLA Ops:
  6.5 30.1 %all-gather.3.cloned.1.call-start = ((), (), s32[]{:S(2)}) async-start(), calls=%async_computation | async-start | bytes 12582912 | tf_op jit(solution)/shard_map/all_gather | solution.py:33
  7.4 2.2 %copy-start = (bf16[2048,1024]{1,0:T(8,128)(2,1)S(1)}, bf16[2048,1024]{1,0:T(8,128)(2,1)}, u32[]{:S(2)}) copy-start(bf16[2048,1024]{1,0:T(8,128)(2,1)} %param.5) | copy-start | bytes 12582916
  9.6 5.2 %copy-start.1 = (bf16[256,2048]{1,0:T(8,128)(2,1)S(1)}, bf16[256,2048]{1,0:T(8,128)(2,1)}, u32[]{:S(2)}) copy-start(bf16[256,2048]{1,0:T(8,128)(2,1)} %param.6) | copy-start | bytes 3145732
  13.9 151.0 %all-gather.5.cloned.1.call-start = ((), (), s32[]{:S(2)}) async-start(), calls=%async_computation.1 | async-start | bytes 9437184 | tf_op jit(solution)/shard_map/all_gather | solution.py:36
Sparse Core Ops, SparseCore 0:
  14.0 22.5 all-gather.2
  38.7 126.0 all-gather.4
where the time goes:
time: 196 us
  waiting for transfers between devices  149 us (76%)
  matrix products  24.6 us (13%)
  between operations  13.5 us (7%)
  other arithmetic  6.81 us (3%)
  local copies, waits for them, and re-layouts  2.38 us (1%)
    all_gather x1, waiting for transfers between devices, on_device(): lax.all_gather(b_kept, 'row', axis=0, tiled=True)  128 us
    dot_general x1, matrix products, on_device(): jnp.dot(a_whole, lax.all_gather(b_kept, 'row', axis=0, tiled=True), prefe...  24.6 us
    all_gather x1, waiting for transfers between devices, on_device(): a_whole = lax.all_gather(a_kept, 'col', axis=1, tiled=True)  20.7 us
    mul x2, other arithmetic, expand(): kept = shaped * flags[:, None, :, None].astype(source.dtype)  5.28 us
  transfers between devices with their start and end apart: 2, of which 2 were waited for; matrix products, arithmetic and copies ran while one was open for 1% of the time, Pallas kernels for 0%

commit v1 on v0

v1 whole, which is shorter than its diff:
```python
import functools

import jax
import jax.numpy as jnp
from jax import lax
from jax.experimental import pallas as pl
from jax.experimental.pallas import tpu as pltpu
from jax.sharding import PartitionSpec as P

TW = 256
PANEL = 512
ROWS = 256


def ring_of(n):
    if n == 8:
        return [0, 2, 4, 6, 7, 5, 3, 1]
    return list(range(n))


def body(place, a_mask, b_mask, *refs, offsets, panel, first_row, base_wide, out_wide, chained):
    count = len(offsets)
    own_ref, other_ref = refs[:2]
    blocks = refs[2 : 2 + count]
    base_ref = refs[2 + count]
    out_ref, parts, total = refs[3 + count + chained :]
    step = pl.program_id(0)
    depth = blocks[0].shape[0]
    half = own_ref.shape[1]
    per_half = half // depth
    for index in range(per_half):
        parts[index] = own_ref[:, index * depth : (index + 1) * depth]
        parts[per_half + index] = other_ref[:, index * depth : (index + 1) * depth]
    total[...] = base_ref[...].astype(jnp.float32)
    tile_row = place[0] + first_row // TW + step * (ROWS // TW)
    for slot, offset in enumerate(offsets):
        owner = place[2 + offset]
        tile_k = owner * depth // TW
        where = lax.rem(owner + (2 - place[1]) * per_half, 2 * per_half)
        for j in range(PANEL // TW):
            flag = a_mask[tile_row, tile_k] * b_mask[tile_k, place[1] * 8 + panel * (PANEL // TW) + j]

            @pl.when(flag != 0)
            def _():
                total[:, j * TW : (j + 1) * TW] += jnp.dot(
                    parts[where],
                    blocks[slot][:, j * TW : (j + 1) * TW],
                    preferred_element_type=jnp.float32,
                )

    out_ref[...] = total[...].astype(out_ref.dtype)


def multiply(place, a_mask, b_mask, own, other, blocks, base, out, *, panel, first_row, row_count, base_wide, out_wide, width):
    offsets = tuple(sorted(blocks))
    height = own.shape[0]
    skip = first_row // ROWS
    arrays, specs = [], []
    for offset in offsets:
        array = blocks[offset]
        arrays.append(array)
        column = panel if array.shape[1] != PANEL else 0
        specs.append(pl.BlockSpec((array.shape[0], PANEL), functools.partial(lambda c, i, *_: (0, c), column)))
    depth = arrays[0].shape[0]
    base_column = 0 if base_wide else panel
    in_specs = [
        pl.BlockSpec((ROWS, own.shape[1]), lambda i, *_: (i + skip, 0)),
        pl.BlockSpec((ROWS, own.shape[1]), lambda i, *_: (i + skip, 0)),
        *specs,
        pl.BlockSpec((ROWS, PANEL), lambda i, *_: (i + (0 if base_wide else skip), base_column)),
    ]
    operands = [place, a_mask, b_mask, own, other, *arrays, base]
    aliases = {}
    if out_wide:
        out_shape = jax.ShapeDtypeStruct((row_count, PANEL), jnp.float32)
        out_spec = pl.BlockSpec((ROWS, PANEL), lambda i, *_: (i, 0))
    else:
        out_shape = jax.ShapeDtypeStruct((height, width), jnp.bfloat16)
        out_spec = pl.BlockSpec((ROWS, PANEL), lambda i, *_: (i + skip, panel))
    chained = out is not None
    if chained:
        aliases = {len(operands): 0}
        operands.append(out)
        in_specs.append(pl.BlockSpec(memory_space=pl.ANY))
    flops = 2 * row_count * PANEL * depth * len(offsets)
    return pl.pallas_call(
        functools.partial(
            body, offsets=offsets, panel=panel, first_row=first_row, base_wide=base_wide, out_wide=out_wide, chained=chained
        ),
        grid_spec=pltpu.PrefetchScalarGridSpec(
            num_scalar_prefetch=3,
            grid=(row_count // ROWS,),
            in_specs=in_specs,
            out_specs=out_spec,
            scratch_shapes=[
                pltpu.VMEM((2 * own.shape[1] // depth, ROWS, depth), jnp.bfloat16),
                pltpu.VMEM((ROWS, PANEL), jnp.float32),
            ],
        ),
        out_shape=out_shape,
        input_output_aliases=aliases,
        cost_estimate=pl.CostEstimate(flops=flops, bytes_accessed=row_count * 6000, transcendentals=0),
        compiler_params=pltpu.CompilerParams(vmem_limit_bytes=24 * 1024 * 1024),
    )(*operands)


def on_device(n, a_tiles, b_tiles, a_mask, b_mask, c_given):
    ring = ring_of(n)
    right = [(ring[i], ring[(i + 1) % n]) for i in range(n)]
    left = [(t, s) for s, t in right]
    row = lax.axis_index("row")
    col = lax.axis_index("col")
    height, width = c_given.shape
    far = n // 2

    b_panels = [b_tiles[:, p * PANEL : (p + 1) * PANEL] for p in range(width // PANEL)]
    blocks = [{0: b_tiles} for _ in b_panels]
    other = None
    for first in range(0, len(b_panels), 2):
        for hop in range(1, far + 1):
            for which in range(2):
                p = first + which
                for sign, pairs, keep in ((-1, right, 0), (1, left, 1)):
                    if hop == far and which != keep:
                        continue
                    p = first + (which if sign < 0 else 1 - which)
                    if hop == far:
                        p = first + keep
                    source = b_panels[p] if hop == 1 else blocks[p][sign * (hop - 1)]
                    blocks[p][sign * hop] = lax.ppermute(source, "row", pairs)
        if other is None:
            other = lax.ppermute(a_tiles, "col", [(0, 1), (1, 0)])

    ring_array = jnp.array(ring, jnp.int32)
    position = jnp.argmax(ring_array == row).astype(jnp.int32)
    owners = ring_array[(position + jnp.arange(n, dtype=jnp.int32)) % n]
    place = jnp.concatenate([jnp.stack([row * (height // TW), col]).astype(jnp.int32), owners])

    def shift(table):
        return {(offset if offset >= 0 else n + offset): array for offset, array in table.items()}

    call = functools.partial(multiply, place, a_mask, b_mask, a_tiles, other, width=width)
    out = None
    half = height // 2
    for p in range(len(b_panels)):
        last = p >= len(b_panels) - 2
        table = shift(blocks[p])
        for first_row in (0, half):
            settings = dict(panel=p, first_row=first_row, row_count=half)
            if not last:
                out = call(table, c_given, out, base_wide=False, out_wide=False, **settings)
                continue
            early = {k: v for k, v in table.items() if k != far}
            wide = call(early, c_given, None, base_wide=False, out_wide=True, **settings)
            out = call({far: table[far]}, wide, out, base_wide=True, out_wide=False, **settings)
    return out


def solution(mesh):
    return jax.shard_map(
        functools.partial(on_device, mesh.shape["row"]),
        mesh=mesh,
        in_specs=(
            P(("grp", "row"), "col"),
            P(("grp", "row"), "col"),
            P("grp", None),
            P("grp", None),
            P(("grp", "row"), "col"),
        ),
        out_specs=P(("grp", "row"), "col"),
        check_vma=False,
    )
```

time: 196 us -> 180 us (0.918)
  the two profiles are of different devices: /device:TPU:0 before, /device:TPU:16 now
where the time goes in v1:
time: 180 us; the launch traced here: 178 us
  Pallas kernels  102 us (57%)
  waiting for transfers between devices  35.7 us (20%)
  starting transfers between devices  27.4 us (15%)
  local copies, waits for them, and re-layouts  10.8 us (6%)
  other arithmetic  2.06 us (1%)
    pallas_call x12, Pallas kernels, multiply(): pl.pallas_call(functools.partial(body, offsets=offsets, panel=panel, firs...  102 us
    ppermute x28, waiting for transfers between devices, on_device(): blocks[p][sign * hop] = lax.ppermute(source, 'row', pairs)  35.7 us
    ppermute x28, starting transfers between devices, on_device(): blocks[p][sign * hop] = lax.ppermute(source, 'row', pairs)  27.4 us
    unnamed x17, local copies, waits for them, and re-layouts  8.28 us
  transfers between devices with their start and end apart: 29, of which 11 were waited for; matrix products, arithmetic and copies ran while one was open for 3% of the time, Pallas kernels for 51%

profile of v1, /device:TPU:16, one launch (start us, length us, event | category | flops | bytes accessed | tf_op | source)
XLA Modules:
  0.0 178.0 jit_solution(13938109787892754869)
XLA Ops:
  5.4 5.0 %collective-permute-done.25.refs_9_ = bf16[256,512]{1,0:T(8,128)(2,1)S(1)} collective-permute-done((bf16[256,512]{1,0:T(8,128)(2,1)S(1)}, bf16[256,512]{1,0:T(8,128)(2,1)S(1)}, u32[]{:S(2)}, u32[]{:S(2)}) %collective-permute-start.25) | collective-permute-done | bytes 262176 | tf_op jit(solution)/shard_map/ppermute | solution.py:130
  12.5 5.2 %collective-permute-done.15.refs_3_ = bf16[256,512]{1,0:T(8,128)(2,1)S(1)} collective-permute-done((bf16[256,512]{1,0:T(8,128)(2,1)S(1)}, bf16[256,512]{1,0:T(8,128)(2,1)S(1)}, u32[]{:S(2)}, u32[]{:S(2)}) %collective-permute-start.15) | collective-permute-done | bytes 262176 | tf_op jit(solution)/shard_map/ppermute | solution.py:130
  19.7 2.0 %collective-permute-done.8.refs_8_ = bf16[256,512]{1,0:T(8,128)(2,1)S(1)} collective-permute-done((bf16[256,512]{1,0:T(8,128)(2,1)S(1)}, bf16[256,512]{1,0:T(8,128)(2,1)S(1)}, u32[]{:S(2)}, u32[]{:S(2)}) %collective-permute-start.8) | collective-permute-done | bytes 262176 | tf_op jit(solution)/shard_map/ppermute | solution.py:130
  23.7 5.2 %collective-permute-done.1.refs_3_ = bf16[256,512]{1,0:T(8,128)(2,1)S(1)} collective-permute-done((bf16[256,512]{1,0:T(8,128)(2,1)S(1)}, bf16[256,512]{1,0:T(8,128)(2,1)S(1)}, u32[]{:S(2)}, u32[]{:S(2)}) %collective-permute-start.1) | collective-permute-done | bytes 262176 | tf_op jit(solution)/shard_map/ppermute | solution.py:130
  30.9 2.2 %collective-permute-done.26.refs_8_ = bf16[256,512]{1,0:T(8,128)(2,1)} collective-permute-done((bf16[256,512]{1,0:T(8,128)(2,1)S(1)}, bf16[256,512]{1,0:T(8,128)(2,1)}, u32[]{:S(2)}, u32[]{:S(2)}) %collective-permute-start.26) | collective-permute-done | bytes 262176 | tf_op jit(solution)/shard_map/ppermute | solution.py:130
  35.1 5.0 %collective-permute-done.16.refs_4_ = bf16[256,512]{1,0:T(8,128)(2,1)S(1)} collective-permute-done((bf16[256,512]{1,0:T(8,128)(2,1)S(1)}, bf16[256,512]{1,0:T(8,128)(2,1)S(1)}, u32[]{:S(2)}, u32[]{:S(2)}) %collective-permute-start.16) | collective-permute-done | bytes 262176 | tf_op jit(solution)/shard_map/ppermute | solution.py:130
  46.2 3.3 %collective-permute-done.27.refs_7_ = bf16[256,512]{1,0:T(8,128)(2,1)} collective-permute-done((bf16[256,512]{1,0:T(8,128)(2,1)}, bf16[256,512]{1,0:T(8,128)(2,1)}, u32[]{:S(2)}, u32[]{:S(2)}) %collective-permute-start.27) | collective-permute-done | bytes 262176 | tf_op jit(solution)/shard_map/ppermute | solution.py:130
  55.4 2.6 %collective-permute-done.24.refs_5_ = bf16[256,512]{1,0:T(8,128)(2,1)} collective-permute-done((bf16[256,512]{1,0:T(8,128)(2,1)}, bf16[256,512]{1,0:T(8,128)(2,1)}, u32[]{:S(2)}, u32[]{:S(2)}) %collective-permute-start.24) | collective-permute-done | bytes 262176 | tf_op jit(solution)/shard_map/ppermute | solution.py:130
  58.6 3.4 %collective-permute-done.17.refs_5_ = bf16[256,512]{1,0:T(8,128)(2,1)} collective-permute-done((bf16[256,512]{1,0:T(8,128)(2,1)S(1)}, bf16[256,512]{1,0:T(8,128)(2,1)}, u32[]{:S(2)}, u32[]{:S(2)}) %collective-permute-start.17) | collective-permute-done | bytes 262176 | tf_op jit(solution)/shard_map/ppermute | solution.py:130
  64.5 2.2 %copy-done = bf16[2048,1024]{1,0:T(8,128)(2,1)S(1)} copy-done((bf16[2048,1024]{1,0:T(8,128)(2,1)S(1)}, bf16[2048,1024]{1,0:T(8,128)(2,1)}, u32[]{:S(2)}) %copy-start) | copy-done | bytes 4194328
  66.7 3.4 %copy-done.1 = bf16[2048,2048]{1,0:T(8,128)(2,1)S(1)} copy-done((bf16[2048,2048]{1,0:T(8,128)(2,1)S(1)}, bf16[2048,2048]{1,0:T(8,128)(2,1)}, u32[]{:S(2)}) %copy-start.1) | copy-done | bytes 8388632
  72.0 9.2 %shard_map.68.refs_11_ = bf16[2048,2048]{1,0:T(8,128)(2,1)} custom-call(s32[10]{0:T(128)S(1)} %pad_add_fusion.place, s32[64,8]{1,0:T(8,128)S(1)} %copy.37.a_mask, s32[8,16]{1,0:T(8,128)S(1)} %copy-done.4, bf16[2048,1024]{1,0:T(8,128)(2,1)S(1)} %copy-done, bf16[2048,1024]{1,0:T(8,128)(2,1)} %collective-permute-done.refs_1_, bf16[256,2048]{1,0:T(8,128)(2,1)S(1)} %copy-done.2, ...), custom_call_target="tpu_custom_call" | custom-call | flops 2147483648 | bytes 6144000 | tf_op jit(solution)/shard_map/pallas_call | solution.py:86
  81.2 9.3 %shard_map.69.refs_11_ = bf16[2048,2048]{1,0:T(8,128)(2,1)} custom-call(s32[10]{0:T(128)S(1)} %pad_add_fusion.place, s32[64,8]{1,0:T(8,128)S(1)} %copy.37.a_mask, s32[8,16]{1,0:T(8,128)S(1)} %copy-done.4, bf16[2048,1024]{1,0:T(8,128)(2,1)S(1)} %copy-done, bf16[2048,1024]{1,0:T(8,128)(2,1)} %collective-permute-done.refs_1_, ...), custom_call_target="tpu_custom_call", output_to_operand_aliasing={{}: (14, {})} | custom-call | flops 2147483648 | bytes 6144000 | tf_op jit(solution)/shard_map/pallas_call | solution.py:86
  90.6 2.0 %collective-permute-start.7 = (bf16[256,512]{1,0:T(8,128)(2,1)S(1)}, bf16[256,512]{1,0:T(8,128)(2,1)S(1)}, u32[]{:S(2)}, u32[]{:S(2)}) collective-permute-start(bf16[256,512]{1,0:T(8,128)(2,1)S(1)} %collective-permute-done.6.refs_7_), channel_id=1, source_target_pairs={{0,4},{4,8},{8,12},{12,14},{14,10},{10,6},{6,2},{2,0},{1,5},{5,9},... | collective-permute-start | bytes 786440 | tf_op jit(solution)/shard_map/ppermute | solution.py:130
  94.6 10.7 %shard_map.70.refs_11_ = bf16[2048,2048]{1,0:T(8,128)(2,1)} custom-call(s32[10]{0:T(128)S(1)} %pad_add_fusion.place, s32[64,8]{1,0:T(8,128)S(1)} %copy.37.a_mask, s32[8,16]{1,0:T(8,128)S(1)} %copy-done.4, bf16[2048,1024]{1,0:T(8,128)(2,1)S(1)} %copy-done, bf16[2048,1024]{1,0:T(8,128)(2,1)} %collective-permute-done.refs_1_, ...), custom_call_target="tpu_custom_call", output_to_operand_aliasing={{}: (14, {})} | custom-call | flops 2147483648 | bytes 6144000 | tf_op jit(solution)/shard_map/pallas_call | solution.py:86
  105.3 12.5 %shard_map.71.refs_4_ = bf16[2048,2048]{1,0:T(8,128)(2,1)} custom-call(s32[10]{0:T(128)S(1)} %pad_add_fusion.place, s32[64,8]{1,0:T(8,128)S(1)} %copy.37.a_mask, s32[8,16]{1,0:T(8,128)S(1)} %copy-done.4, bf16[2048,1024]{1,0:T(8,128)(2,1)S(1)} %copy-done, bf16[2048,1024]{1,0:T(8,128)(2,1)} %collective-permute-done.refs_1_, ...), custom_call_target="tpu_custom_call", output_to_operand_aliasing={{}: (14, {})} | custom-call | flops 2147483648 | bytes 6144000 | tf_op jit(solution)/shard_map/pallas_call | solution.py:86
  117.8 9.2 %shard_map.67.refs_3_ = f32[1024,512]{1,0:T(8,128)S(1)} custom-call(s32[10]{0:T(128)S(1)} %pad_add_fusion.place, s32[64,8]{1,0:T(8,128)S(1)} %copy.37.a_mask, s32[8,16]{1,0:T(8,128)S(1)} %copy-done.5, bf16[2048,1024]{1,0:T(8,128)(2,1)S(1)} %copy-done, bf16[2048,1024]{1,0:T(8,128)(2,1)} %collective-permute-done.refs_1_, bf16[256,2048]{1,0:T(8,128)(2,1)S(1)} %copy-done.2, ...), custom_call_target="tpu_custom_call" | custom-call | flops 1879048192 | bytes 6144000 | tf_op jit(solution)/shard_map/pallas_call | solution.py:86
  127.0 9.6 %shard_map.66.refs_3_ = f32[1024,512]{1,0:T(8,128)S(1)} custom-call(s32[10]{0:T(128)S(1)} %pad_add_fusion.place, s32[64,8]{1,0:T(8,128)S(1)} %copy.37.a_mask, s32[8,16]{1,0:T(8,128)S(1)} %copy-done.5, bf16[2048,1024]{1,0:T(8,128)(2,1)S(1)} %copy-done, bf16[2048,1024]{1,0:T(8,128)(2,1)} %collective-permute-done.refs_1_, bf16[256,2048]{1,0:T(8,128)(2,1)S(1)} %copy-done.2, ...), custom_call_target="tpu_custom_call" | custom-call | flops 1879048192 | bytes 6144000 | tf_op jit(solution)/shard_map/pallas_call | solution.py:86
  136.7 9.6 %shard_map.65.refs_3_ = f32[1024,512]{1,0:T(8,128)S(1)} custom-call(s32[10]{0:T(128)S(1)} %pad_add_fusion.place, s32[64,8]{1,0:T(8,128)S(1)} %copy.37.a_mask, s32[8,16]{1,0:T(8,128)S(1)} %copy-done.5, bf16[2048,1024]{1,0:T(8,128)(2,1)S(1)} %copy-done, bf16[2048,1024]{1,0:T(8,128)(2,1)} %collective-permute-done.refs_1_, bf16[256,2048]{1,0:T(8,128)(2,1)S(1)} %copy-done.2, ...), custom_call_target="tpu_custom_call" | custom-call | flops 1879048192 | bytes 6144000 | tf_op jit(solution)/shard_map/pallas_call | solution.py:86
  146.3 5.0 %shard_map.72.refs_4_ = bf16[2048,2048]{1,0:T(8,128)(2,1)} custom-call(s32[10]{0:T(128)S(1)} %pad_add_fusion.place, s32[64,8]{1,0:T(8,128)S(1)} %copy.37.a_mask, s32[8,16]{1,0:T(8,128)S(1)} %copy-done.5, bf16[2048,1024]{1,0:T(8,128)(2,1)S(1)} %copy-done, bf16[2048,1024]{1,0:T(8,128)(2,1)} %collective-permute-done.refs_1_, ...), custom_call_target="tpu_custom_call", output_to_operand_aliasing={{}: (7, {})} | custom-call | flops 268435456 | bytes 6144000 | tf_op jit(solution)/shard_map/pallas_call | solution.py:86
  151.3 5.7 %shard_map.73.refs_4_ = bf16[2048,2048]{1,0:T(8,128)(2,1)} custom-call(s32[10]{0:T(128)S(1)} %pad_add_fusion.place, s32[64,8]{1,0:T(8,128)S(1)} %copy.37.a_mask, s32[8,16]{1,0:T(8,128)S(1)} %copy-done.5, bf16[2048,1024]{1,0:T(8,128)(2,1)S(1)} %copy-done, bf16[2048,1024]{1,0:T(8,128)(2,1)} %collective-permute-done.refs_1_, ...), custom_call_target="tpu_custom_call", output_to_operand_aliasing={{}: (7, {})} | custom-call | flops 268435456 | bytes 6144000 | tf_op jit(solution)/shard_map/pallas_call | solution.py:86
  157.0 10.4 %shard_map.64.refs_3_ = f32[1024,512]{1,0:T(8,128)S(1)} custom-call(s32[10]{0:T(128)S(1)} %pad_add_fusion.place, s32[64,8]{1,0:T(8,128)S(1)} %copy.37.a_mask, s32[8,16]{1,0:T(8,128)S(1)} %copy-done.5, bf16[2048,1024]{1,0:T(8,128)(2,1)S(1)} %copy-done, bf16[2048,1024]{1,0:T(8,128)(2,1)} %collective-permute-done.refs_1_, bf16[256,2048]{1,0:T(8,128)(2,1)S(1)} %copy-done.3, ...), custom_call_target="tpu_custom_call" | custom-call | flops 1879048192 | bytes 6144000 | tf_op jit(solution)/shard_map/pallas_call | solution.py:86
  167.4 5.0 %shard_map.74.refs_4_ = bf16[2048,2048]{1,0:T(8,128)(2,1)} custom-call(s32[10]{0:T(128)S(1)} %pad_add_fusion.place, s32[64,8]{1,0:T(8,128)S(1)} %copy.37.a_mask, s32[8,16]{1,0:T(8,128)S(1)} %copy-done.5, bf16[2048,1024]{1,0:T(8,128)(2,1)S(1)} %copy-done, bf16[2048,1024]{1,0:T(8,128)(2,1)} %collective-permute-done.refs_1_, ...), custom_call_target="tpu_custom_call", output_to_operand_aliasing={{}: (7, {})} | custom-call | flops 268435456 | bytes 6144000 | tf_op jit(solution)/shard_map/pallas_call | solution.py:86
  172.3 5.7 %shard_map.75 = bf16[2048,2048]{1,0:T(8,128)(2,1)} custom-call(s32[10]{0:T(128)S(1)} %pad_add_fusion.place, s32[64,8]{1,0:T(8,128)S(1)} %copy.37.a_mask, s32[8,16]{1,0:T(8,128)S(1)} %copy-done.5, bf16[2048,1024]{1,0:T(8,128)(2,1)S(1)} %copy-done, bf16[2048,1024]{1,0:T(8,128)(2,1)} %collective-permute-done.refs_1_, ...), custom_call_target="tpu_custom_call", output_to_operand_aliasing={{}: (7, {})} | custom-call | flops 268435456 | bytes 6144000 | tf_op jit(solution)/shard_map/pallas_call | solution.py:86
  (70 shorter events, 34.7 us)
Async XLA Ops:
  0.0 64.0 %collective-permute-start = (bf16[2048,1024]{1,0:T(8,128)(2,1)}, bf16[2048,1024]{1,0:T(8,128)(2,1)}, u32[]{:S(2)}, u32[]{:S(2)}) collective-permute-start(bf16[2048,1024]{1,0:T(8,128)(2,1)} %refs_0_.23), channel_id=1, source_target_pairs={{0,1},{1,0},{2,3},{3,2},{4,5},{5,4},{6,7},{7,6},{8,9},{9,8},{10,11... | collective-permute-start | bytes 12582920 | tf_op jit(solution)/shard_map/ppermute | solution.py:132
  3.3 14.3 %collective-permute-start.15 = (bf16[256,512]{1,0:T(8,128)(2,1)S(1)}, bf16[256,512]{1,0:T(8,128)(2,1)S(1)}, u32[]{:S(2)}, u32[]{:S(2)}) collective-permute-start(bf16[256,512]{1,0:T(8,128)(2,1)S(1)} %get-tuple-element.8), channel_id=1, source_target_pairs={{4,0},{8,4},{12,8},{14,12},{10,14},{6,10},{2,6},{0,2},{5,1},{9,5},... | collective-permute-start | bytes 786440 | tf_op jit(solution)/shard_map/ppermute | solution.py:130
  3.8 14.3 %collective-permute-start.19 = (bf16[256,512]{1,0:T(8,128)(2,1)S(1)}, bf16[256,512]{1,0:T(8,128)(2,1)S(1)}, u32[]{:S(2)}, u32[]{:S(2)}) collective-permute-start(bf16[256,512]{1,0:T(8,128)(2,1)S(1)} %get-tuple-element.8), channel_id=1, source_target_pairs={{0,4},{4,8},{8,12},{12,14},{14,10},{10,6},{6,2},{2,0},{1,5},{5,9},... | collective-permute-start | bytes 786440 | tf_op jit(solution)/shard_map/ppermute | solution.py:130
  10.4 11.2 %collective-permute-start.8 = (bf16[256,512]{1,0:T(8,128)(2,1)S(1)}, bf16[256,512]{1,0:T(8,128)(2,1)S(1)}, u32[]{:S(2)}, u32[]{:S(2)}) collective-permute-start(bf16[256,512]{1,0:T(8,128)(2,1)S(1)} %get-tuple-element.9), channel_id=1, source_target_pairs={{0,4},{4,8},{8,12},{12,14},{14,10},{10,6},{6,2},{2,0},{1,5},{5,9},... | collective-permute-start | bytes 786440 | tf_op jit(solution)/shard_map/ppermute | solution.py:130
  12.0 11.2 %collective-permute-start.12 = (bf16[256,512]{1,0:T(8,128)(2,1)S(1)}, bf16[256,512]{1,0:T(8,128)(2,1)S(1)}, u32[]{:S(2)}, u32[]{:S(2)}) collective-permute-start(bf16[256,512]{1,0:T(8,128)(2,1)S(1)} %get-tuple-element.9), channel_id=1, source_target_pairs={{4,0},{8,4},{12,8},{14,12},{10,14},{6,10},{2,6},{0,2},{5,1},{9,5},... | collective-permute-start | bytes 786440 | tf_op jit(solution)/shard_map/ppermute | solution.py:130
  17.7 11.2 %collective-permute-start.1 = (bf16[256,512]{1,0:T(8,128)(2,1)S(1)}, bf16[256,512]{1,0:T(8,128)(2,1)S(1)}, u32[]{:S(2)}, u32[]{:S(2)}) collective-permute-start(bf16[256,512]{1,0:T(8,128)(2,1)S(1)} %get-tuple-element.10), channel_id=1, source_target_pairs={{4,0},{8,4},{12,8},{14,12},{10,14},{6,10},{2,6},{0,2},{5,1},{9,5},... | collective-permute-start | bytes 786440 | tf_op jit(solution)/shard_map/ppermute | solution.py:130
  18.1 11.2 %collective-permute-start.5 = (bf16[256,512]{1,0:T(8,128)(2,1)S(1)}, bf16[256,512]{1,0:T(8,128)(2,1)S(1)}, u32[]{:S(2)}, u32[]{:S(2)}) collective-permute-start(bf16[256,512]{1,0:T(8,128)(2,1)S(1)} %get-tuple-element.10), channel_id=1, source_target_pairs={{0,4},{4,8},{8,12},{12,14},{14,10},{10,6},{6,2},{2,0},{1,5},{5,9},... | collective-permute-start | bytes 786440 | tf_op jit(solution)/shard_map/ppermute | solution.py:130
  21.7 11.4 %collective-permute-start.26 = (bf16[256,512]{1,0:T(8,128)(2,1)S(1)}, bf16[256,512]{1,0:T(8,128)(2,1)}, u32[]{:S(2)}, u32[]{:S(2)}) collective-permute-start(bf16[256,512]{1,0:T(8,128)(2,1)S(1)} %collective-permute-done.25.refs_9_), channel_id=1, source_target_pairs={{0,4},{4,8},{8,12},{12,14},{14,10},{10,6},{6,2},{2,0},{1,5},{5,9},... | collective-permute-start | bytes 786440 | tf_op jit(solution)/shard_map/ppermute | solution.py:130
  23.3 11.4 %collective-permute-start.23 = (bf16[256,512]{1,0:T(8,128)(2,1)S(1)}, bf16[256,512]{1,0:T(8,128)(2,1)}, u32[]{:S(2)}, u32[]{:S(2)}) collective-permute-start(bf16[256,512]{1,0:T(8,128)(2,1)S(1)} %collective-permute-done.22.refs_3_), channel_id=1, source_target_pairs={{4,0},{8,4},{12,8},{14,12},{10,14},{6,10},{2,6},{0,2},{5,1},{9,5},... | collective-permute-start | bytes 786440 | tf_op jit(solution)/shard_map/ppermute | solution.py:130
  28.9 11.2 %collective-permute-start.16 = (bf16[256,512]{1,0:T(8,128)(2,1)S(1)}, bf16[256,512]{1,0:T(8,128)(2,1)S(1)}, u32[]{:S(2)}, u32[]{:S(2)}) collective-permute-start(bf16[256,512]{1,0:T(8,128)(2,1)S(1)} %collective-permute-done.15.refs_3_), channel_id=1, source_target_pairs={{4,0},{8,4},{12,8},{14,12},{10,14},{6,10},{2,6},{0,2},{5,1},{9,5},... | collective-permute-start | bytes 786440 | tf_op jit(solution)/shard_map/ppermute | solution.py:130
  29.3 13.6 %collective-permute-start.20 = (bf16[256,512]{1,0:T(8,128)(2,1)S(1)}, bf16[256,512]{1,0:T(8,128)(2,1)S(1)}, u32[]{:S(2)}, u32[]{:S(2)}) collective-permute-start(bf16[256,512]{1,0:T(8,128)(2,1)S(1)} %collective-permute-done.19.refs_9_), channel_id=1, source_target_pairs={{0,4},{4,8},{8,12},{12,14},{14,10},{10,6},{6,2},{2,0},{1,5},{5,9},... | collective-permute-start | bytes 786440 | tf_op jit(solution)/shard_map/ppermute | solution.py:130
  33.1 11.1 %collective-permute-start.9 = (bf16[256,512]{1,0:T(8,128)(2,1)S(1)}, bf16[256,512]{1,0:T(8,128)(2,1)S(1)}, u32[]{:S(2)}, u32[]{:S(2)}) collective-permute-start(bf16[256,512]{1,0:T(8,128)(2,1)S(1)} %collective-permute-done.8.refs_8_), channel_id=1, source_target_pairs={{0,4},{4,8},{8,12},{12,14},{14,10},{10,6},{6,2},{2,0},{1,5},{5,9},... | collective-permute-start | bytes 786440 | tf_op jit(solution)/shard_map/ppermute | solution.py:130
  44.2 13.7 %collective-permute-start.24 = (bf16[256,512]{1,0:T(8,128)(2,1)}, bf16[256,512]{1,0:T(8,128)(2,1)}, u32[]{:S(2)}, u32[]{:S(2)}) collective-permute-start(bf16[256,512]{1,0:T(8,128)(2,1)} %collective-permute-done.23.refs_4_), channel_id=1, source_target_pairs={{4,0},{8,4},{12,8},{14,12},{10,14},{6,10},{2,6},{0,2},{5,1},{9,5},... | collective-permute-start | bytes 786440 | tf_op jit(solution)/shard_map/ppermute | solution.py:130
  45.7 16.3 %collective-permute-start.17 = (bf16[256,512]{1,0:T(8,128)(2,1)S(1)}, bf16[256,512]{1,0:T(8,128)(2,1)}, u32[]{:S(2)}, u32[]{:S(2)}) collective-permute-start(bf16[256,512]{1,0:T(8,128)(2,1)S(1)} %collective-permute-done.16.refs_4_), channel_id=1, source_target_pairs={{4,0},{8,4},{12,8},{14,12},{10,14},{6,10},{2,6},{0,2},{5,1},{9,5},... | collective-permute-start | bytes 786440 | tf_op jit(solution)/shard_map/ppermute | solution.py:130
  49.5 14.1 %collective-permute-start.28 = (bf16[256,512]{1,0:T(8,128)(2,1)}, bf16[256,512]{1,0:T(8,128)(2,1)}, u32[]{:S(2)}, u32[]{:S(2)}) collective-permute-start(bf16[256,512]{1,0:T(8,128)(2,1)} %collective-permute-done.27.refs_7_), channel_id=1, source_target_pairs={{0,4},{4,8},{8,12},{12,14},{14,10},{10,6},{6,2},{2,0},{1,5},{5,9},... | collective-permute-start | bytes 786440 | tf_op jit(solution)/shard_map/ppermute | solution.py:130
  53.9 36.7 %collective-permute-start.6 = (bf16[256,512]{1,0:T(8,128)(2,1)S(1)}, bf16[256,512]{1,0:T(8,128)(2,1)S(1)}, u32[]{:S(2)}, u32[]{:S(2)}) collective-permute-start(bf16[256,512]{1,0:T(8,128)(2,1)S(1)} %collective-permute-done.5.refs_8_), channel_id=1, source_target_pairs={{0,4},{4,8},{8,12},{12,14},{14,10},{10,6},{6,2},{2,0},{1,5},{5,9},... | collective-permute-start | bytes 786440 | tf_op jit(solution)/shard_map/ppermute | solution.py:130
  58.0 32.6 %collective-permute-start.21 = (bf16[256,512]{1,0:T(8,128)(2,1)S(1)}, bf16[256,512]{1,0:T(8,128)(2,1)S(1)}, u32[]{:S(2)}, u32[]{:S(2)}) collective-permute-start(bf16[256,512]{1,0:T(8,128)(2,1)S(1)} %collective-permute-done.20.refs_8_), channel_id=1, source_target_pairs={{0,4},{4,8},{8,12},{12,14},{14,10},{10,6},{6,2},{2,0},{1,5},{5,9},... | collective-permute-start | bytes 786440 | tf_op jit(solution)/shard_map/ppermute | solution.py:130
  62.0 30.6 %collective-permute-start.10 = (bf16[256,512]{1,0:T(8,128)(2,1)S(1)}, bf16[256,512]{1,0:T(8,128)(2,1)S(1)}, u32[]{:S(2)}, u32[]{:S(2)}) collective-permute-start(bf16[256,512]{1,0:T(8,128)(2,1)S(1)} %collective-permute-done.9.refs_7_), channel_id=1, source_target_pairs={{0,4},{4,8},{8,12},{12,14},{14,10},{10,6},{6,2},{2,0},{1,5},{5,9},... | collective-permute-start | bytes 786440 | tf_op jit(solution)/shard_map/ppermute | solution.py:130
  63.5 29.5 %collective-permute-start.3 = (bf16[256,512]{1,0:T(8,128)(2,1)S(1)}, bf16[256,512]{1,0:T(8,128)(2,1)S(1)}, u32[]{:S(2)}, u32[]{:S(2)}) collective-permute-start(bf16[256,512]{1,0:T(8,128)(2,1)S(1)} %collective-permute-done.2.refs_4_), channel_id=1, source_target_pairs={{4,0},{8,4},{12,8},{14,12},{10,14},{6,10},{2,6},{0,2},{5,1},{9,5},... | collective-permute-start | bytes 786440 | tf_op jit(solution)/shard_map/ppermute | solution.py:130
  64.0 30.6 %collective-permute-start.18 = (bf16[256,512]{1,0:T(8,128)(2,1)}, bf16[256,512]{1,0:T(8,128)(2,1)S(1)}, u32[]{:S(2)}, u32[]{:S(2)}) collective-permute-start(bf16[256,512]{1,0:T(8,128)(2,1)} %collective-permute-done.17.refs_5_), channel_id=1, source_target_pairs={{4,0},{8,4},{12,8},{14,12},{10,14},{6,10},{2,6},{0,2},{5,1},{9,5},... | collective-permute-start | bytes 786440 | tf_op jit(solution)/shard_map/ppermute | solution.py:130
  90.5 27.3 %collective-permute-start.14 = (bf16[256,512]{1,0:T(8,128)(2,1)S(1)}, bf16[256,512]{1,0:T(8,128)(2,1)S(1)}, u32[]{:S(2)}, u32[]{:S(2)}) collective-permute-start(bf16[256,512]{1,0:T(8,128)(2,1)S(1)} %collective-permute-done.13.refs_4_), channel_id=1, source_target_pairs={{4,0},{8,4},{12,8},{14,12},{10,14},{6,10},{2,6},{0,2},{5,1},{9,5},... | collective-permute-start | bytes 786440 | tf_op jit(solution)/shard_map/ppermute | solution.py:130
  90.6 46.1 %collective-permute-start.7 = (bf16[256,512]{1,0:T(8,128)(2,1)S(1)}, bf16[256,512]{1,0:T(8,128)(2,1)S(1)}, u32[]{:S(2)}, u32[]{:S(2)}) collective-permute-start(bf16[256,512]{1,0:T(8,128)(2,1)S(1)} %collective-permute-done.6.refs_7_), channel_id=1, source_target_pairs={{0,4},{4,8},{8,12},{12,14},{14,10},{10,6},{6,2},{2,0},{1,5},{5,9},... | collective-permute-start | bytes 786440 | tf_op jit(solution)/shard_map/ppermute | solution.py:130
  92.6 53.7 %collective-permute-start.11 = (bf16[256,512]{1,0:T(8,128)(2,1)S(1)}, bf16[256,512]{1,0:T(8,128)(2,1)S(1)}, u32[]{:S(2)}, u32[]{:S(2)}) collective-permute-start(bf16[256,512]{1,0:T(8,128)(2,1)S(1)} %collective-permute-done.10.refs_6_), channel_id=1, source_target_pairs={{0,4},{4,8},{8,12},{12,14},{14,10},{10,6},{6,2},{2,0},{1,5},{5,9},... | collective-permute-start | bytes 786440 | tf_op jit(solution)/shard_map/ppermute | solution.py:130
  93.0 74.3 %collective-permute-start.4 = (bf16[256,512]{1,0:T(8,128)(2,1)S(1)}, bf16[256,512]{1,0:T(8,128)(2,1)S(1)}, u32[]{:S(2)}, u32[]{:S(2)}) collective-permute-start(bf16[256,512]{1,0:T(8,128)(2,1)S(1)} %collective-permute-done.3.refs_5_), channel_id=1, source_target_pairs={{4,0},{8,4},{12,8},{14,12},{10,14},{6,10},{2,6},{0,2},{5,1},{9,5},... | collective-permute-start | bytes 786440 | tf_op jit(solution)/shard_map/ppermute | solution.py:130
  (13 other events, 103.8 us)

commit v2 on v0

v2 whole, which is shorter than its diff:
```python
import collections
import functools

import jax
import jax.numpy as jnp
from jax import lax
from jax.experimental import pallas as pl
from jax.experimental.pallas import tpu as pltpu
from jax.sharding import PartitionSpec as P

TW = 256
ROWS = 512
MIB = 1024 * 1024
VMEM = 20 * MIB


def ring_of(n):
    if n == 8:
        return [0, 2, 4, 6, 7, 5, 3, 1]
    return list(range(n))


def prepare_body(place, a_mask, own_ref, other_ref, out_ref, *, depth, n):
    per_half = n // 2
    tiles = own_ref.shape[0] // TW
    for tile in range(tiles):
        rows = slice(tile * TW, (tile + 1) * TW)
        tile_row = place[0] + pl.program_id(0) * tiles + tile
        for away, ref in enumerate((own_ref, other_ref)):
            first = lax.rem(place[1] + away, 2) * per_half
            for index in range(per_half):
                owner = first + index
                flag = a_mask[tile_row, owner * depth // TW].astype(out_ref.dtype)
                out_ref[place[2 + n + owner], rows, :] = ref[rows, index * depth : (index + 1) * depth] * flag


def prepare(place, a_mask, own, other, n):
    height, half = own.shape
    depth = 2 * half // n
    return pl.pallas_call(
        functools.partial(prepare_body, depth=depth, n=n),
        grid_spec=pltpu.PrefetchScalarGridSpec(
            num_scalar_prefetch=2,
            grid=(height // ROWS,),
            in_specs=[pl.BlockSpec((ROWS, half), lambda i, *_: (i, 0))] * 2,
            out_specs=pl.BlockSpec((n, ROWS, depth), lambda i, *_: (0, i, 0)),
        ),
        out_shape=pltpu.VMEM((n, height, depth), jnp.bfloat16),
        cost_estimate=pl.CostEstimate(flops=0, bytes_accessed=height * half // 16, transcendentals=0),
        compiler_params=pltpu.CompilerParams(vmem_limit_bytes=VMEM),
    )(place, a_mask, own, other)


def multiply_body(place, b_mask, *refs, layout, low, high, first, chained):
    left, refs = refs[: high - low], refs[high - low :]
    blocks = refs[: len(layout)]
    base_ref = refs[len(layout)]
    out_ref, kept = refs[len(layout) + 1 + chained :]
    depth = blocks[0].shape[0]

    @pl.when(pl.program_id(0) == 0)
    def _():
        for ref, (slot, shift) in zip(blocks, layout):
            tile_k = place[2 + slot] * depth // TW
            for j in range(ref.shape[1] // TW):
                at = shift + j * TW
                flag = b_mask[tile_k, place[1] * 8 + (first + at) // TW].astype(kept.dtype)
                block = ref[:, j * TW : (j + 1) * TW]
                kept[(slot - low) * depth : (slot - low + 1) * depth, at : at + TW] = block * flag

    left = [ref[0] for ref in left]
    left = jnp.concatenate(left, axis=1) if len(left) > 1 else left[0]
    product = jnp.dot(left, kept[...], preferred_element_type=jnp.float32)
    out_ref[...] = (base_ref[...].astype(jnp.float32) + product).astype(out_ref.dtype)


def multiply(place, b_mask, a_kept, arrived, base, base_column, out, *, low, high, first, size, wide, width):
    height = a_kept.shape[1]
    depth = arrived[0][2].shape[0]
    operands = [place, b_mask] + [a_kept] * (high - low)
    whole = pl.BlockSpec(memory_space=pltpu.VMEM)
    in_specs = [
        pl.BlockSpec((1, ROWS, depth), functools.partial(lambda slot, i, *_: (slot, i, 0), slot)) for slot in range(low, high)
    ]
    for _, _, array in arrived:
        operands.append(array)
        if array.shape[1] == width:
            in_specs.append(pl.BlockSpec((depth, size), lambda i, *_: (0, first // size)))
        else:
            in_specs.append(whole)
    operands.append(base)
    in_specs.append(pl.BlockSpec((ROWS, size), lambda i, *_: (i, base_column // size)))
    if wide:
        out_shape = pltpu.VMEM((height, size), jnp.float32)
        out_spec = pl.BlockSpec((ROWS, size), lambda i, *_: (i, 0))
    else:
        out_shape = jax.ShapeDtypeStruct((height, width), jnp.bfloat16)
        out_spec = pl.BlockSpec((ROWS, size), lambda i, *_: (i, first // size))
    aliases = {}
    if out is not None:
        aliases = {len(operands): 0}
        operands.append(pltpu.with_memory_space_constraint(out, pltpu.HBM))
        in_specs.append(pl.BlockSpec(memory_space=pl.ANY))
    extent = (high - low) * depth
    return pl.pallas_call(
        functools.partial(
            multiply_body,
            layout=tuple((slot, shift) for slot, shift, _ in arrived),
            low=low,
            high=high,
            first=first,
            chained=out is not None,
        ),
        grid_spec=pltpu.PrefetchScalarGridSpec(
            num_scalar_prefetch=2,
            grid=(height // ROWS,),
            in_specs=in_specs,
            out_specs=out_spec,
            scratch_shapes=[pltpu.VMEM((extent, size), jnp.bfloat16)],
        ),
        out_shape=out_shape,
        input_output_aliases=aliases,
        cost_estimate=pl.CostEstimate(
            flops=height * size * extent // 16, bytes_accessed=height * size // 16, transcendentals=0
        ),
        compiler_params=pltpu.CompilerParams(vmem_limit_bytes=VMEM),
    )(*operands)


def on_device(n, a_tiles, b_tiles, a_mask, b_mask, c_given):
    ring = ring_of(n)
    right = [(ring[i], ring[(i + 1) % n]) for i in range(n)]
    left = [(t, s) for s, t in right]
    row = lax.axis_index("row")
    col = lax.axis_index("col")
    height, width = c_given.shape
    far = n // 2
    panel = width // 2

    offsets = [0] + [sign * hop for hop in range(1, far) for sign in (-1, 1)] + [far]
    table = []
    for r in range(n):
        owners = [ring[(ring.index(r) + o) % n] for o in offsets]
        table.append(owners + [owners.index(owner) for owner in range(n)])
    table = lax.dynamic_index_in_dim(jnp.array(table, jnp.int32), row, 0, keepdims=False)
    place = jnp.concatenate([jnp.stack([row * (height // TW), col]).astype(jnp.int32), table])

    rounds = [(p, hop, 0, panel) for hop in range(1, far) for p in range(2)]
    rounds += [(0, far, 0, panel), (1, far, 0, panel)]
    work = collections.defaultdict(list)
    last = len(rounds)
    work[last - 4] = [(0, 0, n - 3, 0, panel)]
    work[last - 3] = [(1, 0, n - 3, 0, panel)]
    work[last - 2] = [(0, n - 3, n - 1, 0, panel)]
    work[last] = [(1, n - 3, n - 1, 0, panel), (0, n - 1, n, 0, panel), (1, n - 1, n, 0, panel)]

    blocks = [{0: b_tiles} for _ in range(2)]
    other = a_kept = out = None
    wide = {}
    tied = []
    for index in range(last + 1):
        if index < last:
            p, hop, start, stop = rounds[index]
            sources = []
            for sign in (-1, 1):
                if hop == 1:
                    source = b_tiles[:, p * panel : (p + 1) * panel]
                else:
                    source = blocks[p][sign * (hop - 1)]
                if hop == far:
                    middle = (start + stop) // 2
                    source = source[:, start:middle] if sign < 0 else source[:, middle:stop]
                sources.append(source)
            if tied:
                *sources, _ = lax.optimization_barrier((*sources, tied))
            tied = []
            for sign, pairs, source in zip((-1, 1), (right, left), sources):
                key = (sign * hop, start) if hop == far else sign * hop
                blocks[p][key] = lax.ppermute(source, "row", pairs)
        if index == 0:
            other = lax.ppermute(a_tiles, "col", [(0, 1), (1, 0)])
        if index == 1:
            source = pltpu.with_memory_space_constraint(a_tiles, pltpu.HBM)
            a_kept = prepare(place, a_mask, source, other, n)
            tied.append(a_kept)
        for p, low, high, start, stop in work[index]:
            arrived = []
            for slot in range(low, high):
                if offsets[slot] == far:
                    arrived.append((slot, 0, blocks[p][-far, start]))
                    arrived.append((slot, (stop - start) // 2, blocks[p][far, start]))
                else:
                    arrived.append((slot, 0, blocks[p][offsets[slot]]))
            done = high == n
            if low:
                base, base_column = wide[p], start
            else:
                base, base_column = pltpu.with_memory_space_constraint(c_given, pltpu.HBM), p * panel + start
            result = multiply(
                place, b_mask, a_kept, arrived, base, base_column, out if done else None,
                low=low, high=high, first=p * panel + start, size=stop - start, wide=not done, width=width,
            )
            tied.append(result)
            if done:
                out = result
            else:
                wide[p] = result
    return out


def solution(mesh):
    return jax.shard_map(
        functools.partial(on_device, mesh.shape["row"]),
        mesh=mesh,
        in_specs=(
            P(("grp", "row"), "col"),
            P(("grp", "row"), "col"),
            P("grp", None),
            P("grp", None),
            P(("grp", "row"), "col"),
        ),
        out_specs=P(("grp", "row"), "col"),
        check_vma=False,
    )
```

time: 196 us -> 91 us (0.46)
  waiting for transfers between devices: 149 us -> 31.6 us
  Pallas kernels: 0 us -> 38 us
  matrix products: 24.6 us -> 0 us
  starting transfers between devices: 0.04 us -> 17.3 us
  between operations: 13.5 us -> 0.13 us
  other arithmetic: 6.81 us -> 0.08 us
    all_gather x2 -> x0, waiting for transfers between devices: 149 us -> none  [the longest x1 128 us: on_device(): lax.all_gather(b_kept, 'row', axis=0, tiled=True)]
    pallas_call x0 -> x7, Pallas kernels: none -> 38 us  [the longest x6 32.4 us: multiply(): pl.pallas_call(functools.partial(multiply_body, layout=tuple(((slot, shif...]
    ppermute x0 -> x17, waiting for transfers between devices: none -> 31.6 us  [the longest x16 31.6 us: on_device(): blocks[p][key] = lax.ppermute(source, 'row', pairs)]
    dot_general x1 -> x0, matrix products: 24.6 us -> none  [on_device(): jnp.dot(a_whole, lax.all_gather(b_kept, 'row', axis=0, tiled=True), prefe...]
    ppermute x0 -> x17, starting transfers between devices: none -> 17.3 us  [the longest x16 16.8 us: on_device(): blocks[p][key] = lax.ppermute(source, 'row', pairs)]
    mul x2 -> x0, other arithmetic: 5.28 us -> none  [expand(): kept = shaped * flags[:, None, :, None].astype(source.dtype)]
    slice x0 -> x5, local copies, waits for them, and re-layouts: none -> 2.13 us  [the longest x1 2.06 us: on_device(): source = b_tiles[:, p * panel:(p + 1) * panel]]
  transfers between devices with their start and end apart: 2 -> 17, of which waited for: 2 -> 8; matrix products, arithmetic and copies ran while one was open for 1% -> 4% of each run, Pallas kernels for 0% -> 38%
where the time goes in v2:
time: 91 us; the launch traced here: 90.7 us
  Pallas kernels  38 us (42%)
  waiting for transfers between devices  31.6 us (35%)
  starting transfers between devices  17.3 us (19%)
  local copies, waits for them, and re-layouts  3.6 us (4%)
    pallas_call x6, Pallas kernels, multiply(): pl.pallas_call(functools.partial(multiply_body, layout=tuple(((slot, shif...  32.4 us
    ppermute x16, waiting for transfers between devices, on_device(): blocks[p][key] = lax.ppermute(source, 'row', pairs)  31.6 us
    ppermute x16, starting transfers between devices, on_device(): blocks[p][key] = lax.ppermute(source, 'row', pairs)  16.8 us
    pallas_call x1, Pallas kernels, prepare(): pl.pallas_call(functools.partial(prepare_body, depth=depth, n=n), grid_sp...  5.62 us
    slice x1, local copies, waits for them, and re-layouts, on_device(): source = b_tiles[:, p * panel:(p + 1) * panel]  2.06 us
  transfers between devices with their start and end apart: 17, of which 8 were waited for; matrix products, arithmetic and copies ran while one was open for 4% of the time, Pallas kernels for 38%

profile of v2, /device:TPU:0, one launch (start us, length us, event | category | flops | bytes accessed | tf_op | source)
XLA Modules:
  0.0 90.7 jit_solution(14725810880446256443)
XLA Ops:
  0.5 2.1 %fusion = (bf16[256,1024]{1,0:T(8,128)(2,1)}, bf16[256,1024]{1,0:T(8,128)(2,1)S(1)}) fusion(bf16[256,2048]{1,0:T(8,128)(2,1)} %refs_5_.3), kind=kLoop, calls=%fused_computation.2 | loop fusion | bytes 2097152 | tf_op jit(solution)/shard_map/slice | solution.py:167
  2.5 2.5 %collective-permute-start.6 = (bf16[256,1024]{1,0:T(8,128)(2,1)}, bf16[256,1024]{1,0:T(8,128)(2,1)S(1)}, u32[]{:S(2)}, u32[]{:S(2)}) collective-permute-start(bf16[256,1024]{1,0:T(8,128)(2,1)} %get-tuple-element.21), channel_id=1, source_target_pairs={{4,0},{8,4},{12,8},{14,12},{10,14},{6,10},{2,6},{0,2},{5,1},{9,5},... | collective-permute-start | bytes 1572872 | tf_op jit(solution)/shard_map/ppermute | solution.py:179
  5.1 2.0 %collective-permute-start.3 = (bf16[256,1024]{1,0:T(8,128)(2,1)S(1)}, bf16[256,1024]{1,0:T(8,128)(2,1)S(1)}, u32[]{:S(2)}, u32[]{:S(2)}) collective-permute-start(bf16[256,1024]{1,0:T(8,128)(2,1)S(1)} %get-tuple-element.22), channel_id=1, source_target_pairs={{4,0},{8,4},{12,8},{14,12},{10,14},{6,10},{2,6},{0,2},{5,1},{9,5},... | collective-permute-start | bytes 1572872 | tf_op jit(solution)/shard_map/ppermute | solution.py:179
  7.1 0.8 copy.8.a_mask
  8.7 5.6 %shard_map.64.refs_0_.refs_1_.refs_2_.refs_3_.refs_4_ = bf16[8,2048,256]{2,1,0:T(8,128)(2,1)S(1)} custom-call(s32[18]{0:T(128)S(1)} %pad_add_fusion.place, s32[64,8]{1,0:T(8,128)S(1)} %copy.8.a_mask, bf16[2048,1024]{1,0:T(8,128)(2,1)} %own_ref.1, bf16[2048,1024]{1,0:T(8,128)(2,1)} %collective-permute-done.other_ref), custom_call_target="tpu_custom_call" | custom-call | bytes 131072 | tf_op jit(solution)/shard_map/pallas_call | solution.py:40
  14.3 3.8 %collective-permute-done.6.refs_7_ = bf16[256,1024]{1,0:T(8,128)(2,1)S(1)} collective-permute-done((bf16[256,1024]{1,0:T(8,128)(2,1)}, bf16[256,1024]{1,0:T(8,128)(2,1)S(1)}, u32[]{:S(2)}, u32[]{:S(2)}) %collective-permute-start.6) | collective-permute-done | bytes 524320 | tf_op jit(solution)/shard_map/ppermute | solution.py:179
  18.1 1.9 %collective-permute-done.5.refs_6_ = bf16[256,1024]{1,0:T(8,128)(2,1)S(1)} collective-permute-done((bf16[256,1024]{1,0:T(8,128)(2,1)}, bf16[256,1024]{1,0:T(8,128)(2,1)S(1)}, u32[]{:S(2)}, u32[]{:S(2)}) %collective-permute-start.5) | collective-permute-done | bytes 524320 | tf_op jit(solution)/shard_map/ppermute | solution.py:179
  20.0 2.0 %collective-permute-start.8 = (bf16[256,1024]{1,0:T(8,128)(2,1)S(1)}, bf16[256,1024]{1,0:T(8,128)(2,1)S(1)}, u32[]{:S(2)}, u32[]{:S(2)}) collective-permute-start(bf16[256,1024]{1,0:T(8,128)(2,1)S(1)} %collective-permute-done.6.refs_7_), channel_id=1, source_target_pairs={{4,0},{8,4},{12,8},{14,12},{10,14},{6,10},{2,6},{0,2},{5,1},{9,5},... | collective-permute-start | bytes 1572872 | tf_op jit(solution)/shard_map/ppermute | solution.py:179
  22.0 7.3 %collective-permute-done.3.refs_7_ = bf16[256,1024]{1,0:T(8,128)(2,1)S(1)} collective-permute-done((bf16[256,1024]{1,0:T(8,128)(2,1)S(1)}, bf16[256,1024]{1,0:T(8,128)(2,1)S(1)}, u32[]{:S(2)}, u32[]{:S(2)}) %collective-permute-start.3) | collective-permute-done | bytes 524320 | tf_op jit(solution)/shard_map/ppermute | solution.py:179
  29.3 1.9 %collective-permute-start.4 = (bf16[256,1024]{1,0:T(8,128)(2,1)S(1)}, bf16[256,1024]{1,0:T(8,128)(2,1)S(1)}, u32[]{:S(2)}, u32[]{:S(2)}) collective-permute-start(bf16[256,1024]{1,0:T(8,128)(2,1)S(1)} %collective-permute-done.3.refs_7_), channel_id=1, source_target_pairs={{4,0},{8,4},{12,8},{14,12},{10,14},{6,10},{2,6},{0,2},{5,1},{9,5},... | collective-permute-start | bytes 1572872 | tf_op jit(solution)/shard_map/ppermute | solution.py:179
  31.3 11.1 %collective-permute-done.7.refs_8_ = bf16[256,1024]{1,0:T(8,128)(2,1)S(1)} collective-permute-done((bf16[256,1024]{1,0:T(8,128)(2,1)S(1)}, bf16[256,1024]{1,0:T(8,128)(2,1)S(1)}, u32[]{:S(2)}, u32[]{:S(2)}) %collective-permute-start.7) | collective-permute-done | bytes 524320 | tf_op jit(solution)/shard_map/ppermute | solution.py:179
  42.5 2.0 %collective-permute-start.12 = (bf16[256,1024]{1,0:T(8,128)(2,1)S(1)}, bf16[256,1024]{1,0:T(8,128)(2,1)S(1)}, u32[]{:S(2)}, u32[]{:S(2)}) collective-permute-start(bf16[256,1024]{1,0:T(8,128)(2,1)S(1)} %collective-permute-done.8.refs_9_), channel_id=1, source_target_pairs={{4,0},{8,4},{12,8},{14,12},{10,14},{6,10},{2,6},{0,2},{5,1},{9,5},... | collective-permute-start | bytes 1572872 | tf_op jit(solution)/shard_map/ppermute | solution.py:179
  44.5 8.5 %shard_map.65.refs_4_ = f32[2048,1024]{1,0:T(8,128)S(1)} custom-call(s32[18]{0:T(128)S(1)} %pad_add_fusion.place, s32[8,16]{1,0:T(8,128)S(1)} %copy-done.1, bf16[8,2048,256]{2,1,0:T(8,128)(2,1)S(1)} %shard_map.64.refs_0_.refs_1_.refs_2_.refs_3_.refs_4_, bf16[8,2048,256]{2,1,0:T(8,128)(2,1)S(1)} %shard_map.64.refs_0_.refs_1_.refs_2_.refs_3_.refs_4_, ...), custom_call_target="tpu_custom_call" | custom-call | flops 167772160 | bytes 131072 | tf_op jit(solution)/shard_map/pallas_call | solution.py:105
  53.0 0.7 collective-permute-done.2.refs_8_
  53.7 2.0 %collective-permute-start.10 = (bf16[256,1024]{1,0:T(8,128)(2,1)S(1)}, bf16[256,1024]{1,0:T(8,128)(2,1)S(1)}, u32[]{:S(2)}, u32[]{:S(2)}) collective-permute-start(bf16[256,1024]{1,0:T(8,128)(2,1)S(1)} %collective-permute-done.4.refs_9_), channel_id=1, source_target_pairs={{4,0},{8,4},{12,8},{14,12},{10,14},{6,10},{2,6},{0,2},{5,1},{9,5},... | collective-permute-start | bytes 1572872 | tf_op jit(solution)/shard_map/ppermute | solution.py:179
  55.7 8.5 %shard_map.67.refs_4_ = f32[2048,1024]{1,0:T(8,128)S(1)} custom-call(s32[18]{0:T(128)S(1)} %pad_add_fusion.place, s32[8,16]{1,0:T(8,128)S(1)} %copy-done.1, bf16[8,2048,256]{2,1,0:T(8,128)(2,1)S(1)} %shard_map.64.refs_0_.refs_1_.refs_2_.refs_3_.refs_4_, bf16[8,2048,256]{2,1,0:T(8,128)(2,1)S(1)} %shard_map.64.refs_0_.refs_1_.refs_2_.refs_3_.refs_4_, ...), custom_call_target="tpu_custom_call" | custom-call | flops 167772160 | bytes 131072 | tf_op jit(solution)/shard_map/pallas_call | solution.py:105
  64.2 0.7 collective-permute-done.11.refs_2_
  65.1 2.0 %collective-permute-start.16 = (bf16[256,512]{1,0:T(8,128)(2,1)S(1)}, bf16[256,512]{1,0:T(8,128)(2,1)S(1)}, u32[]{:S(2)}, u32[]{:S(2)}) collective-permute-start(bf16[256,512]{1,0:T(8,128)(2,1)S(1)} %slice.29), channel_id=1, source_target_pairs={{4,0},{8,4},{12,8},{14,12},{10,14},{6,10},{2,6},{0,2},{5,1},{9,5},... | collective-permute-start | bytes 786440 | tf_op jit(solution)/shard_map/ppermute | solution.py:179
  67.1 3.7 %shard_map.66.refs_3_ = f32[2048,1024]{1,0:T(8,128)S(1)} custom-call(s32[18]{0:T(128)S(1)} %pad_add_fusion.place, s32[8,16]{1,0:T(8,128)S(1)} %copy-done.1, bf16[8,2048,256]{2,1,0:T(8,128)(2,1)S(1)} %shard_map.64.refs_0_.refs_1_.refs_2_.refs_3_.refs_4_, bf16[8,2048,256]{2,1,0:T(8,128)(2,1)S(1)} %shard_map.64.refs_0_.refs_1_.refs_2_.refs_3_.refs_4_, ...), custom_call_target="tpu_custom_call" | custom-call | flops 67108864 | bytes 131072 | tf_op jit(solution)/shard_map/pallas_call | solution.py:105
  70.8 5.4 %collective-permute-done.9.refs_2_ = bf16[256,1024]{1,0:T(8,128)(2,1)S(1)} collective-permute-done((bf16[256,1024]{1,0:T(8,128)(2,1)S(1)}, bf16[256,1024]{1,0:T(8,128)(2,1)S(1)}, u32[]{:S(2)}, u32[]{:S(2)}) %collective-permute-start.9) | collective-permute-done | bytes 524320 | tf_op jit(solution)/shard_map/ppermute | solution.py:179
  76.3 2.0 %collective-permute-start.14 = (bf16[256,512]{1,0:T(8,128)(2,1)S(1)}, bf16[256,512]{1,0:T(8,128)(2,1)S(1)}, u32[]{:S(2)}, u32[]{:S(2)}) collective-permute-start(bf16[256,512]{1,0:T(8,128)(2,1)S(1)} %slice.27), channel_id=1, source_target_pairs={{4,0},{8,4},{12,8},{14,12},{10,14},{6,10},{2,6},{0,2},{5,1},{9,5},... | collective-permute-start | bytes 786440 | tf_op jit(solution)/shard_map/ppermute | solution.py:179
  78.3 3.7 %shard_map.68.refs_3_ = f32[2048,1024]{1,0:T(8,128)S(1)} custom-call(s32[18]{0:T(128)S(1)} %pad_add_fusion.place, s32[8,16]{1,0:T(8,128)S(1)} %copy-done.1, bf16[8,2048,256]{2,1,0:T(8,128)(2,1)S(1)} %shard_map.64.refs_0_.refs_1_.refs_2_.refs_3_.refs_4_, bf16[8,2048,256]{2,1,0:T(8,128)(2,1)S(1)} %shard_map.64.refs_0_.refs_1_.refs_2_.refs_3_.refs_4_, ...), custom_call_target="tpu_custom_call" | custom-call | flops 67108864 | bytes 131072 | tf_op jit(solution)/shard_map/pallas_call | solution.py:105
  82.1 4.0 %shard_map.69.refs_4_ = bf16[2048,2048]{1,0:T(8,128)(2,1)} custom-call(s32[18]{0:T(128)S(1)} %pad_add_fusion.place, s32[8,16]{1,0:T(8,128)S(1)} %copy-done.1, bf16[8,2048,256]{2,1,0:T(8,128)(2,1)S(1)} %shard_map.64.refs_0_.refs_1_.refs_2_.refs_3_.refs_4_, bf16[256,512]{1,0:T(8,128)(2,1)S(1)} %collective-permute-done.15.refs_1_, ...), custom_call_target="tpu_custom_call" | custom-call | flops 33554432 | bytes 131072 | tf_op jit(solution)/shard_map/pallas_call | solution.py:105
  86.7 4.0 %shard_map.70 = bf16[2048,2048]{1,0:T(8,128)(2,1)} custom-call(s32[18]{0:T(128)S(1)} %pad_add_fusion.place, s32[8,16]{1,0:T(8,128)S(1)} %copy-done.1, bf16[8,2048,256]{2,1,0:T(8,128)(2,1)S(1)} %shard_map.64.refs_0_.refs_1_.refs_2_.refs_3_.refs_4_, bf16[256,512]{1,0:T(8,128)(2,1)S(1)} %collective-permute-done.13.refs_1_, ...), custom_call_target="tpu_custom_call", output_to_operand_aliasing={{}: (6, {})} | custom-call | flops 33554432 | bytes 131072 | tf_op jit(solution)/shard_map/pallas_call | solution.py:105
  (29 shorter events, 2.5 us)
Async XLA Ops:
  0.0 8.7 %collective-permute-start = (bf16[2048,1024]{1,0:T(8,128)(2,1)}, bf16[2048,1024]{1,0:T(8,128)(2,1)}, u32[]{:S(2)}, u32[]{:S(2)}) collective-permute-start(bf16[2048,1024]{1,0:T(8,128)(2,1)} %own_ref.1), channel_id=1, source_target_pairs={{0,1},{1,0},{2,3},{3,2},{4,5},{5,4},{6,7},{7,6},{8,9},{9,8},{10,11... | collective-permute-start | bytes 12582920 | tf_op jit(solution)/shard_map/ppermute | solution.py:181
  2.5 15.6 %collective-permute-start.6 = (bf16[256,1024]{1,0:T(8,128)(2,1)}, bf16[256,1024]{1,0:T(8,128)(2,1)S(1)}, u32[]{:S(2)}, u32[]{:S(2)}) collective-permute-start(bf16[256,1024]{1,0:T(8,128)(2,1)} %get-tuple-element.21), channel_id=1, source_target_pairs={{4,0},{8,4},{12,8},{14,12},{10,14},{6,10},{2,6},{0,2},{5,1},{9,5},... | collective-permute-start | bytes 1572872 | tf_op jit(solution)/shard_map/ppermute | solution.py:179
  5.0 15.0 %collective-permute-start.5 = (bf16[256,1024]{1,0:T(8,128)(2,1)}, bf16[256,1024]{1,0:T(8,128)(2,1)S(1)}, u32[]{:S(2)}, u32[]{:S(2)}) collective-permute-start(bf16[256,1024]{1,0:T(8,128)(2,1)} %get-tuple-element.21), channel_id=1, source_target_pairs={{0,4},{4,8},{8,12},{12,14},{14,10},{10,6},{6,2},{2,0},{1,5},{5,9},... | collective-permute-start | bytes 1572872 | tf_op jit(solution)/shard_map/ppermute | solution.py:179
  5.1 24.2 %collective-permute-start.3 = (bf16[256,1024]{1,0:T(8,128)(2,1)S(1)}, bf16[256,1024]{1,0:T(8,128)(2,1)S(1)}, u32[]{:S(2)}, u32[]{:S(2)}) collective-permute-start(bf16[256,1024]{1,0:T(8,128)(2,1)S(1)} %get-tuple-element.22), channel_id=1, source_target_pairs={{4,0},{8,4},{12,8},{14,12},{10,14},{6,10},{2,6},{0,2},{5,1},{9,5},... | collective-permute-start | bytes 1572872 | tf_op jit(solution)/shard_map/ppermute | solution.py:179
  7.1 24.2 %collective-permute-start.1 = (bf16[256,1024]{1,0:T(8,128)(2,1)S(1)}, bf16[256,1024]{1,0:T(8,128)(2,1)S(1)}, u32[]{:S(2)}, u32[]{:S(2)}) collective-permute-start(bf16[256,1024]{1,0:T(8,128)(2,1)S(1)} %get-tuple-element.22), channel_id=1, source_target_pairs={{0,4},{4,8},{8,12},{12,14},{14,10},{10,6},{6,2},{2,0},{1,5},{5,9},... | collective-permute-start | bytes 1572872 | tf_op jit(solution)/shard_map/ppermute | solution.py:179
  8.7 35.8 %copy-start = (bf16[256,2048]{1,0:T(8,128)(2,1)S(1)}, bf16[256,2048]{1,0:T(8,128)(2,1)}, u32[]{:S(2)}) copy-start(bf16[256,2048]{1,0:T(8,128)(2,1)} %refs_5_.3) | copy-start | bytes 3145732
  8.7 35.8 %copy-start.1 = (s32[8,16]{1,0:T(8,128)S(1)}, s32[8,16]{1,0:T(8,128)}, u32[]{:S(2)}) copy-start(s32[8,16]{1,0:T(8,128)} %b_mask.11) | copy-start | bytes 1540
  20.0 22.5 %collective-permute-start.7 = (bf16[256,1024]{1,0:T(8,128)(2,1)S(1)}, bf16[256,1024]{1,0:T(8,128)(2,1)S(1)}, u32[]{:S(2)}, u32[]{:S(2)}) collective-permute-start(bf16[256,1024]{1,0:T(8,128)(2,1)S(1)} %collective-permute-done.5.refs_6_), channel_id=1, source_target_pairs={{0,4},{4,8},{8,12},{12,14},{14,10},{10,6},{6,2},{2,0},{1,5},{5,9},... | collective-permute-start | bytes 1572872 | tf_op jit(solution)/shard_map/ppermute | solution.py:179
  20.0 22.5 %collective-permute-start.8 = (bf16[256,1024]{1,0:T(8,128)(2,1)S(1)}, bf16[256,1024]{1,0:T(8,128)(2,1)S(1)}, u32[]{:S(2)}, u32[]{:S(2)}) collective-permute-start(bf16[256,1024]{1,0:T(8,128)(2,1)S(1)} %collective-permute-done.6.refs_7_), channel_id=1, source_target_pairs={{4,0},{8,4},{12,8},{14,12},{10,14},{6,10},{2,6},{0,2},{5,1},{9,5},... | collective-permute-start | bytes 1572872 | tf_op jit(solution)/shard_map/ppermute | solution.py:179
  29.3 23.7 %collective-permute-start.4 = (bf16[256,1024]{1,0:T(8,128)(2,1)S(1)}, bf16[256,1024]{1,0:T(8,128)(2,1)S(1)}, u32[]{:S(2)}, u32[]{:S(2)}) collective-permute-start(bf16[256,1024]{1,0:T(8,128)(2,1)S(1)} %collective-permute-done.3.refs_7_), channel_id=1, source_target_pairs={{4,0},{8,4},{12,8},{14,12},{10,14},{6,10},{2,6},{0,2},{5,1},{9,5},... | collective-permute-start | bytes 1572872 | tf_op jit(solution)/shard_map/ppermute | solution.py:179
  31.2 22.5 %collective-permute-start.2 = (bf16[256,1024]{1,0:T(8,128)(2,1)S(1)}, bf16[256,1024]{1,0:T(8,128)(2,1)S(1)}, u32[]{:S(2)}, u32[]{:S(2)}) collective-permute-start(bf16[256,1024]{1,0:T(8,128)(2,1)S(1)} %collective-permute-done.1.refs_6_), channel_id=1, source_target_pairs={{0,4},{4,8},{8,12},{12,14},{14,10},{10,6},{6,2},{2,0},{1,5},{5,9},... | collective-permute-start | bytes 1572872 | tf_op jit(solution)/shard_map/ppermute | solution.py:179
  42.5 22.5 %collective-permute-start.11 = (bf16[256,1024]{1,0:T(8,128)(2,1)S(1)}, bf16[256,1024]{1,0:T(8,128)(2,1)S(1)}, u32[]{:S(2)}, u32[]{:S(2)}) collective-permute-start(bf16[256,1024]{1,0:T(8,128)(2,1)S(1)} %collective-permute-done.7.refs_8_), channel_id=1, source_target_pairs={{0,4},{4,8},{8,12},{12,14},{14,10},{10,6},{6,2},{2,0},{1,5},{5,9},... | collective-permute-start | bytes 1572872 | tf_op jit(solution)/shard_map/ppermute | solution.py:179
  42.5 22.5 %collective-permute-start.12 = (bf16[256,1024]{1,0:T(8,128)(2,1)S(1)}, bf16[256,1024]{1,0:T(8,128)(2,1)S(1)}, u32[]{:S(2)}, u32[]{:S(2)}) collective-permute-start(bf16[256,1024]{1,0:T(8,128)(2,1)S(1)} %collective-permute-done.8.refs_9_), channel_id=1, source_target_pairs={{4,0},{8,4},{12,8},{14,12},{10,14},{6,10},{2,6},{0,2},{5,1},{9,5},... | collective-permute-start | bytes 1572872 | tf_op jit(solution)/shard_map/ppermute | solution.py:179
  53.7 22.5 %collective-permute-start.9 = (bf16[256,1024]{1,0:T(8,128)(2,1)S(1)}, bf16[256,1024]{1,0:T(8,128)(2,1)S(1)}, u32[]{:S(2)}, u32[]{:S(2)}) collective-permute-start(bf16[256,1024]{1,0:T(8,128)(2,1)S(1)} %collective-permute-done.2.refs_8_), channel_id=1, source_target_pairs={{0,4},{4,8},{8,12},{12,14},{14,10},{10,6},{6,2},{2,0},{1,5},{5,9},... | collective-permute-start | bytes 1572872 | tf_op jit(solution)/shard_map/ppermute | solution.py:179
  53.7 22.5 %collective-permute-start.10 = (bf16[256,1024]{1,0:T(8,128)(2,1)S(1)}, bf16[256,1024]{1,0:T(8,128)(2,1)S(1)}, u32[]{:S(2)}, u32[]{:S(2)}) collective-permute-start(bf16[256,1024]{1,0:T(8,128)(2,1)S(1)} %collective-permute-done.4.refs_9_), channel_id=1, source_target_pairs={{4,0},{8,4},{12,8},{14,12},{10,14},{6,10},{2,6},{0,2},{5,1},{9,5},... | collective-permute-start | bytes 1572872 | tf_op jit(solution)/shard_map/ppermute | solution.py:179
  65.0 17.1 %collective-permute-start.15 = (bf16[256,512]{1,0:T(8,128)(2,1)S(1)}, bf16[256,512]{1,0:T(8,128)(2,1)S(1)}, u32[]{:S(2)}, u32[]{:S(2)}) collective-permute-start(bf16[256,512]{1,0:T(8,128)(2,1)S(1)} %slice.28), channel_id=1, source_target_pairs={{0,4},{4,8},{8,12},{12,14},{14,10},{10,6},{6,2},{2,0},{1,5},{5,9},... | collective-permute-start | bytes 786440 | tf_op jit(solution)/shard_map/ppermute | solution.py:179
  65.1 17.0 %collective-permute-start.16 = (bf16[256,512]{1,0:T(8,128)(2,1)S(1)}, bf16[256,512]{1,0:T(8,128)(2,1)S(1)}, u32[]{:S(2)}, u32[]{:S(2)}) collective-permute-start(bf16[256,512]{1,0:T(8,128)(2,1)S(1)} %slice.29), channel_id=1, source_target_pairs={{4,0},{8,4},{12,8},{14,12},{10,14},{6,10},{2,6},{0,2},{5,1},{9,5},... | collective-permute-start | bytes 786440 | tf_op jit(solution)/shard_map/ppermute | solution.py:179
  76.2 10.5 %collective-permute-start.13 = (bf16[256,512]{1,0:T(8,128)(2,1)S(1)}, bf16[256,512]{1,0:T(8,128)(2,1)S(1)}, u32[]{:S(2)}, u32[]{:S(2)}) collective-permute-start(bf16[256,512]{1,0:T(8,128)(2,1)S(1)} %slice.26), channel_id=1, source_target_pairs={{0,4},{4,8},{8,12},{12,14},{14,10},{10,6},{6,2},{2,0},{1,5},{5,9},... | collective-permute-start | bytes 786440 | tf_op jit(solution)/shard_map/ppermute | solution.py:179
  76.3 10.4 %collective-permute-start.14 = (bf16[256,512]{1,0:T(8,128)(2,1)S(1)}, bf16[256,512]{1,0:T(8,128)(2,1)S(1)}, u32[]{:S(2)}, u32[]{:S(2)}) collective-permute-start(bf16[256,512]{1,0:T(8,128)(2,1)S(1)} %slice.27), channel_id=1, source_target_pairs={{4,0},{8,4},{12,8},{14,12},{10,14},{6,10},{2,6},{0,2},{5,1},{9,5},... | collective-permute-start | bytes 786440 | tf_op jit(solution)/shard_map/ppermute | solution.py:179

commit v3 on v2

--- a/solution.py
+++ b/solution.py
@@ -10,8 +10,12 @@
 
 TW = 256
 ROWS = 512
+LAST_ROWS = 1024
 MIB = 1024 * 1024
 VMEM = 20 * MIB
+SEND = 3
+GATHER_VMEM = 16 * MIB
+STEPS_OF = {False: 2, True: 2}
 
 
 def ring_of(n):
@@ -77,10 +81,11 @@
 def multiply(place, b_mask, a_kept, arrived, base, base_column, out, *, low, high, first, size, wide, width):
     height = a_kept.shape[1]
     depth = arrived[0][2].shape[0]
+    rows = LAST_ROWS if high - low == 1 else ROWS
     operands = [place, b_mask] + [a_kept] * (high - low)
     whole = pl.BlockSpec(memory_space=pltpu.VMEM)
     in_specs = [
-        pl.BlockSpec((1, ROWS, depth), functools.partial(lambda slot, i, *_: (slot, i, 0), slot)) for slot in range(low, high)
+        pl.BlockSpec((1, rows, depth), functools.partial(lambda slot, i, *_: (slot, i, 0), slot)) for slot in range(low, high)
     ]
     for _, _, array in arrived:
         operands.append(array)
@@ -89,13 +94,13 @@
         else:
             in_specs.append(whole)
     operands.append(base)
-    in_specs.append(pl.BlockSpec((ROWS, size), lambda i, *_: (i, base_column // size)))
+    in_specs.append(pl.BlockSpec((rows, size), lambda i, *_: (i, base_column // size)))
     if wide:
         out_shape = pltpu.VMEM((height, size), jnp.float32)
-        out_spec = pl.BlockSpec((ROWS, size), lambda i, *_: (i, 0))
+        out_spec = pl.BlockSpec((rows, size), lambda i, *_: (i, 0))
     else:
         out_shape = jax.ShapeDtypeStruct((height, width), jnp.bfloat16)
-        out_spec = pl.BlockSpec((ROWS, size), lambda i, *_: (i, first // size))
+        out_spec = pl.BlockSpec((rows, size), lambda i, *_: (i, first // size))
     aliases = {}
     if out is not None:
         aliases = {len(operands): 0}
@@ -113,7 +118,7 @@
         ),
         grid_spec=pltpu.PrefetchScalarGridSpec(
             num_scalar_prefetch=2,
-            grid=(height // ROWS,),
+            grid=(height // rows,),
             in_specs=in_specs,
             out_specs=out_spec,
             scratch_shapes=[pltpu.VMEM((extent, size), jnp.bfloat16)],
@@ -127,7 +132,19 @@
     )(*operands)
 
 
-def on_device(n, a_tiles, b_tiles, a_mask, b_mask, c_given):
+def places(n, row, col, height):
+    ring = ring_of(n)
+    far = n // 2
+    offsets = [0] + [sign * hop for hop in range(1, far) for sign in (-1, 1)] + [far]
+    table = []
+    for r in range(n):
+        owners = [ring[(ring.index(r) + o) % n] for o in offsets]
+        table.append(owners + [owners.index(owner) for owner in range(n)])
+    table = lax.dynamic_index_in_dim(jnp.array(table, jnp.int32), row, 0, keepdims=False)
+    return offsets, jnp.concatenate([jnp.stack([row * (height // TW), col]).astype(jnp.int32), table])
+
+
+def dense(n, a_tiles, b_tiles, a_mask, b_mask, c_given):
     ring = ring_of(n)
     right = [(ring[i], ring[(i + 1) % n]) for i in range(n)]
     left = [(t, s) for s, t in right]
@@ -137,13 +154,7 @@
     far = n // 2
     panel = width // 2
 
-    offsets = [0] + [sign * hop for hop in range(1, far) for sign in (-1, 1)] + [far]
-    table = []
-    for r in range(n):
-        owners = [ring[(ring.index(r) + o) % n] for o in offsets]
-        table.append(owners + [owners.index(owner) for owner in range(n)])
-    table = lax.dynamic_index_in_dim(jnp.array(table, jnp.int32), row, 0, keepdims=False)
-    place = jnp.concatenate([jnp.stack([row * (height // TW), col]).astype(jnp.int32), table])
+    offsets, place = places(n, row, col, height)
 
     rounds = [(p, hop, 0, panel) for hop in range(1, far) for p in range(2)]
     rounds += [(0, far, 0, panel), (1, far, 0, panel)]
@@ -208,6 +219,336 @@
     return out
 
 
+def pack_body(b_mask, b_hbm, *refs, n, tiles):
+    plan = refs[6]
+    rows, (b_ref, arrived) = refs[7:9], refs[9:]
+    ring = ring_of(n)
+    depth = b_ref.shape[0]
+    fetch = pltpu.make_async_copy(b_hbm, b_ref, arrived)
+    fetch.start()
+    far = n // 2
+    need = jnp.int32(0)
+    for c in range(2):
+        kept = []
+        for owner in ring:
+            total = jnp.int32(0)
+            for j in range(tiles):
+                total += b_mask[owner * depth // TW, c * tiles + j]
+            kept.append(total)
+        span = [jnp.maximum(total, 2 * SEND) for total in kept]
+        for q in range(n):
+            right = sum(span[(q - hop) % n] for hop in range(1, far))
+            left = sum(span[(q + hop) % n] for hop in range(1, far))
+            both = lax.shift_right_logical(right + left + kept[(q + far) % n] + 1, 1)
+            need = jnp.maximum(need, jnp.maximum(jnp.maximum(right, left), both))
+    plan[0] = need
+
+    mine = lax.axis_index("row") * depth // TW
+    half = lax.axis_index("col") * tiles
+    flags = [b_mask[mine, half + j] for j in range(tiles)]
+    total = sum(flags)
+    before = jnp.int32(0)
+    fetch.wait()
+    for j in range(tiles):
+        tile = b_ref[:, j * TW : (j + 1) * TW]
+        dropped = total + j - before
+        rows[0][jnp.where(flags[j] != 0, before, dropped)] = tile
+        rows[1][jnp.where(flags[j] != 0, total - 1 - before, dropped)] = tile
+        before += flags[j]
+    end = jnp.maximum(total, 2 * SEND)
+    plan[1] = 3 * SEND - end
+    for side in range(2):
+        refs[3 * side][...] = rows[side][:SEND]
+        refs[3 * side + 1][...] = rows[side][SEND : 2 * SEND]
+        for i in range(SEND):
+            refs[3 * side + 2][i] = rows[side][end - SEND + i]
+
+
+def pack(b_mask, b_tiles, n):
+    depth, width = b_tiles.shape
+    tiles = width // TW
+    whole = pl.BlockSpec(memory_space=pltpu.VMEM)
+    return pl.pallas_call(
+        functools.partial(pack_body, n=n, tiles=tiles),
+        grid_spec=pltpu.PrefetchScalarGridSpec(
+            num_scalar_prefetch=1,
+            grid=(1,),
+            in_specs=[pl.BlockSpec(memory_space=pl.ANY)],
+            out_specs=[whole] * 6 + [pl.BlockSpec(memory_space=pltpu.SMEM)],
+            scratch_shapes=[pltpu.VMEM((tiles, depth, TW), jnp.bfloat16)] * 2
+            + [pltpu.VMEM((depth, width), jnp.bfloat16), pltpu.SemaphoreType.DMA],
+        ),
+        out_shape=[pltpu.VMEM((SEND, depth, TW), jnp.bfloat16)] * 6 + [jax.ShapeDtypeStruct((2,), jnp.int32)],
+        compiler_params=pltpu.CompilerParams(vmem_limit_bytes=VMEM),
+    )(b_mask, pltpu.with_memory_space_constraint(b_tiles, pltpu.HBM))
+
+
+def choose_body(plan, *refs, count):
+    for before, last, out in (refs[0:2] + refs[4:5], refs[2:4] + refs[5:6]):
+        for start in range(1, SEND + 1):
+
+            @pl.when(plan[1] == start)
+            def _():
+                for i in range(count):
+                    at = start + i
+                    out[i] = before[at] if at < SEND else last[at - SEND]
+
+
+def choose(plan, arrays, count):
+    shape = (count,) + arrays[0].shape[1:]
+    whole = pl.BlockSpec(memory_space=pltpu.VMEM)
+    return pl.pallas_call(
+        functools.partial(choose_body, count=count),
+        grid_spec=pltpu.PrefetchScalarGridSpec(
+            num_scalar_prefetch=1, grid=(1,), in_specs=[whole] * 4, out_specs=[whole] * 2
+        ),
+        out_shape=[pltpu.VMEM(shape, jnp.bfloat16)] * 2,
+        cost_estimate=pl.CostEstimate(flops=0, bytes_accessed=1024, transcendentals=0),
+        compiler_params=pltpu.CompilerParams(vmem_limit_bytes=VMEM),
+    )(plan, *arrays)
+
+
+def gather_multiply_body(
+    place, b_mask, *refs, low, high, carry, carried, limit, offsets, sends_of, tiles, cap, own, final
+):
+    a_ref, refs = refs[0], refs[1:]
+    own_ref, refs = (refs[0], refs[1:]) if own else (None, refs)
+    count = len(sends_of)
+    sends = (refs[:count], refs[count : 2 * count])
+    base_ref, out_ref, kept, store_right, store_left, late = refs[2 * count :]
+    stores = (store_right, store_left)
+    depth = a_ref.shape[2]
+    size = kept.shape[1]
+    far = max(offsets)
+    panel, step = pl.program_id(0), pl.program_id(1)
+    begin = sends_of[0] * SEND if sends_of else 0
+    start = low - carry
+    wide = size // TW
+
+    @pl.when((panel == 0) & (step == 0))
+    def _():
+        for side in range(2):
+            at = 0
+            for ref in sends[side]:
+                stores[side][at : at + ref.shape[0]] = ref[...]
+                at += ref.shape[0]
+
+    @pl.when(step == 0)
+    def _():
+        def row_of(slot):
+            return place[2 + slot] * depth // TW
+
+        totals = {}
+        firsts = {}
+        for slot, offset in enumerate(offsets[:high]):
+            flags = [b_mask[row_of(slot), place[1] * tiles + j] for j in range(tiles)]
+            firsts[offset] = sum(flags[:wide])
+            totals[offset] = firsts[offset] + sum(flags[wide:])
+        waiting = jnp.int32(0)
+        for slot in range(start, high):
+            rows = slice((slot - start) * depth, (slot - start + 1) * depth)
+            offset = offsets[slot]
+            flags = [b_mask[row_of(slot), place[1] * tiles + panel * wide + j] for j in range(wide)]
+            if offset == 0:
+                for j in range(wide):
+                    columns = pl.ds(pl.multiple_of(panel * size + j * TW, TW), TW)
+                    kept[rows, j * TW : (j + 1) * TW] = own_ref[:, columns] * flags[j].astype(kept.dtype)
+                continue
+            total = totals[offset]
+            begins = {}
+            for sign in (-1, 1):
+                begins[sign] = sum(
+                    (jnp.maximum(totals[sign * hop], 2 * SEND) for hop in range(1, abs(offset))), jnp.int32(0)
+                )
+            before = panel * firsts[offset]
+            for j, flag in enumerate(flags):
+                at = (begins[-1] + before, begins[1] + total - 1 - before)
+                columns = slice(j * TW, (j + 1) * TW)
+                if offset == far:
+                    on_right = at[0] < cap
+                    for side, take in ((0, on_right), (1, jnp.logical_not(on_right))):
+                        index = jnp.clip(at[side] - begin, 0, stores[side].shape[0] - 1)
+
+                        @pl.when(take)
+                        def _():
+                            kept[rows, columns] = stores[side][index] * flag.astype(kept.dtype)
+                else:
+                    side = 0 if offset < 0 else 1
+                    valid = flag
+                    if slot < low:
+                        valid = jnp.where(at[side] >= carried, flag, 0)
+                        waiting += valid
+                    elif limit is not None:
+                        valid = jnp.where(at[side] < limit, flag, 0)
+                    index = jnp.clip(at[side] - begin, 0, stores[side].shape[0] - 1)
+                    kept[rows, columns] = stores[side][index] * valid.astype(kept.dtype)
+                before += flag
+        late[0] = waiting
+
+    height = a_ref.shape[1]
+    row_count = height // STEPS_OF[final]
+    rows = pl.ds(pl.multiple_of(step * row_count, row_count), row_count)
+    columns = pl.ds(pl.multiple_of(panel * size, size), size)
+
+    def total_of(from_slot):
+        parts = [a_ref[slot, rows, :] for slot in range(from_slot, high)]
+        parts = jnp.concatenate(parts, axis=1) if len(parts) > 1 else parts[0]
+        product = jnp.dot(parts, kept[(from_slot - start) * depth :, :], preferred_element_type=jnp.float32)
+        base = base_ref[...] if low == 0 else base_ref[rows, columns]
+        total = base.astype(jnp.float32) + product
+        if final:
+            out_ref[...] = total.astype(out_ref.dtype)
+        else:
+            out_ref[rows, columns] = total
+
+    if carry:
+
+        @pl.when(late[0] != 0)
+        def _():
+            total_of(start)
+
+        @pl.when(late[0] == 0)
+        def _():
+            total_of(low)
+
+    else:
+        total_of(low)
+
+
+def gather_multiply(
+    place, b_mask, a_kept, own, sends, base, *, low, high, carry, carried, limit, offsets, sends_of, cap, width
+):
+    height, depth = a_kept.shape[1:]
+    final = high == len(offsets)
+    size = width // 2
+    steps = STEPS_OF[final]
+    rows = height // steps
+    whole = pl.BlockSpec(memory_space=pltpu.VMEM)
+    block = pl.BlockSpec((rows, size), lambda p, i, *_: (i, p))
+    operands = [place, b_mask, a_kept]
+    in_specs = [whole]
+    if own is not None:
+        operands.append(own)
+        in_specs.append(whole)
+    for side in range(2):
+        arrays = [sends[index][side] for index in sends_of]
+        operands += arrays
+        in_specs += [whole] * len(arrays)
+    store = pltpu.VMEM((max(1, sum(array.shape[0] for array in arrays)), depth, TW), jnp.bfloat16)
+    operands.append(base)
+    in_specs.append(whole if low else block)
+    aliases = {}
+    if final:
+        out_shape = jax.ShapeDtypeStruct((height, width), jnp.bfloat16)
+    else:
+        out_shape = pltpu.VMEM((height, width), jnp.float32)
+        if low:
+            aliases = {len(operands) - 1: 0}
+    return pl.pallas_call(
+        functools.partial(
+            gather_multiply_body, low=low, high=high, carry=carry, carried=carried, limit=limit, offsets=offsets,
+            sends_of=sends_of, tiles=width // TW, cap=cap, own=own is not None, final=final,
+        ),
+        grid_spec=pltpu.PrefetchScalarGridSpec(
+            num_scalar_prefetch=2,
+            grid=(2, steps),
+            in_specs=in_specs,
+            out_specs=block if final else whole,
+            scratch_shapes=[
+                pltpu.VMEM(((high - low + carry) * depth, size), jnp.bfloat16), store, store, pltpu.SMEM((1,), jnp.int32)
+            ],
+        ),
+        out_shape=out_shape,
+        input_output_aliases=aliases,
+        cost_estimate=pl.CostEstimate(flops=height * size * depth // 16, bytes_accessed=height * size // 16, transcendentals=0),
+        compiler_params=pltpu.CompilerParams(vmem_limit_bytes=GATHER_VMEM),
+    )(*operands)
+
+
+def sparse(n, cap, a_tiles, b_tiles, a_mask, b_mask, c_given, plan, *packed):
+    ring = ring_of(n)
+    right = [(ring[i], ring[(i + 1) % n]) for i in range(n)]
+    left = [(t, s) for s, t in right]
+    height, width = c_given.shape
+    far = n // 2
+    panel = width // 2
+    tiles = width // TW
+    offsets, place = places(n, lax.axis_index("row"), lax.axis_index("col"), height)
+
+    sizes = [SEND] * (cap // SEND) + ([cap % SEND] if cap % SEND else [])
+    last = len(sizes)
+
+    def sent_by(count):
+        return min(-(-count // SEND), last)
+
+    cut = 1 + 2 * ((far - 1) // 2)
+    near, edge = 2 * far - 3, 2 * far - 1
+    middle = (sent_by(tiles * (far - 2)) - 1) * SEND
+    limit = (last - 1) * SEND
+    phases = [
+        dict(low=0, high=1, carry=0, carried=0, limit=None, sends_of=()),
+        dict(low=1, high=cut, carry=0, carried=0, limit=None, sends_of=(0, sent_by(tiles * (cut // 2)))),
+        dict(low=cut, high=near, carry=0, carried=0, limit=middle, sends_of=(2 * (cut // 2), middle // SEND)),
+        dict(
+            low=near, high=edge, carry=near - cut, carried=middle, limit=limit,
+            sends_of=(min(2 * (far - 2), middle // SEND), last - 1),
+        ),
+        dict(
+            low=edge, high=n, carry=edge - near, carried=limit, limit=None,
+            sends_of=(min(2 * (far - 1), last - 1), last),
+        ),
+    ]
+    work = collections.defaultdict(list)
+    for phase in phases:
+        begin, end = phase["sends_of"] or (0, 2)
+        phase["sends_of"] = tuple(range(begin, end)) if phase["low"] else ()
+        work[min(end + 1, last)].append(phase)
+
+    sends = []
+    tied = []
+    other = a_kept = total = None
+    for index in range(last + 1):
+        if index < last:
+            if index < 2:
+                sources = [packed[index], packed[3 + index]]
+            else:
+                arrays = []
+                for side in range(2):
+                    arrays += [packed[3 * side + 2] if index == 2 else sends[index - 3][side], sends[index - 2][side]]
+                if tied:
+                    *arrays, _ = lax.optimization_barrier((*arrays, tied))
+                    tied = []
+                sources = choose(plan, arrays, sizes[index])
+            sends.append([lax.ppermute(source, "row", pairs) for source, pairs in zip(sources, (right, left))])
+        if index == 0:
+            other = lax.ppermute(a_tiles, "col", [(0, 1), (1, 0)])
+        if index == 1:
+            source = pltpu.with_memory_space_constraint(a_tiles, pltpu.HBM)
+            a_kept = prepare(place, a_mask, source, other, n)
+            tied.append(a_kept)
+        for phase in work[index]:
+            first = phase["low"] == 0
+            total = gather_multiply(
+                place, b_mask, a_kept, b_tiles if first else None, sends,
+                pltpu.with_memory_space_constraint(c_given, pltpu.HBM) if first else total,
+                offsets=tuple(offsets), cap=cap, width=width, **phase,
+            )
+            tied.append(total)
+    return total
+
+
+def on_device(n, *args):
+    b_tiles, b_mask = args[1], args[3]
+    *packed, plan = pack(b_mask, b_tiles, n)
+    tiles = b_tiles.shape[1] // TW
+    most = tiles * (n // 2 - 1) + tiles // 2
+    caps = [most - most * saved // 28 for saved in (4,)]
+    branches = [functools.partial(sparse, n, cap) for cap in caps]
+    branches.append(lambda *operands: dense(n, *operands[:5]))
+    which = sum((plan[0] > cap).astype(jnp.int32) for cap in caps)
+    return lax.switch(which, branches, *args, plan, *packed)
+
+
 def solution(mesh):
     return jax.shard_map(
         functools.partial(on_device, mesh.shape["row"]),

time: 91 us -> 84 us (0.923)
  waiting for transfers between devices: 31.6 us -> 15.4 us
  Pallas kernels: 38 us -> 48.9 us
  local copies, waits for them, and re-layouts: 3.6 us -> 1.47 us
    ppermute x17, waiting for transfers between devices: 31.6 us -> 15.4 us  [the longest x16 14.5 us: sparse(): lax.ppermute(source, 'row', pairs)]
    pallas_call x6 -> x12, Pallas kernels: 32.4 us -> 43.2 us  [the longest x5 36.3 us: gather_multiply(): pl.pallas_call(functools.partial(gather_multiply_body, low=low, high=high...]
    slice x5 -> x0, local copies, waits for them, and re-layouts: 2.13 us -> none  [the longest x1 2.06 us: on_device(): source = b_tiles[:, p * panel:(p + 1) * panel]]
  transfers between devices with their start and end apart: 17 -> 17, of which waited for: 8 -> 7; matrix products, arithmetic and copies ran while one was open for 4% -> 2% of each run, Pallas kernels for 38% -> 47%
where the time goes in v3:
time: 84 us; the launch traced here: 83.7 us
  Pallas kernels  48.9 us (58%)
  starting transfers between devices  17.7 us (21%)
  waiting for transfers between devices  15.4 us (18%)
  local copies, waits for them, and re-layouts  1.47 us (2%)
    pallas_call x5, Pallas kernels, gather_multiply(): pl.pallas_call(functools.partial(gather_multiply_body, low=low, high=high...  36.3 us
    ppermute x16, starting transfers between devices, sparse(): lax.ppermute(source, 'row', pairs)  17.2 us
    ppermute x16, waiting for transfers between devices, sparse(): lax.ppermute(source, 'row', pairs)  14.5 us
    pallas_call x1, Pallas kernels, prepare(): pl.pallas_call(functools.partial(prepare_body, depth=depth, n=n), grid_sp...  5.61 us
    pallas_call x6, Pallas kernels, choose(): pl.pallas_call(functools.partial(choose_body, count=count), grid_spec=plt...  3.79 us
    pallas_call x1, Pallas kernels, pack(): pl.pallas_call(functools.partial(pack_body, n=n, tiles=tiles), grid_spec=...  3.15 us
  transfers between devices with their start and end apart: 17, of which 7 were waited for; matrix products, arithmetic and copies ran while one was open for 2% of the time, Pallas kernels for 47%

profile of v3, /device:TPU:0, one launch (start us, length us, event | category | flops | bytes accessed | tf_op | source)
XLA Modules:
  0.0 83.7 jit_solution(13920281219922631045)
XLA Ops:
  0.0 3.2 %shard_map.75 = (bf16[3,256,256]{2,1,0:T(8,128)(2,1)S(1)}, bf16[3,256,256]{2,1,0:T(8,128)(2,1)S(1)}, bf16[3,256,256]{2,1,0:T(8,128)(2,1)S(1)}, bf16[3,256,256]{2...) custom-call(s32[8,16]{1,0:T(8,128)} %b_mask.1, ...), custom_call_target="tpu_custom_call" | custom-call | tf_op jit(solution)/shard_map/pallas_call | solution.py:271
  3.2 80.5 %conditional.1 = (bf16[2048,2048]{1,0:T(8,128)(2,1)}) conditional(s32[]{:T(128)} %bitcast.6, (s32[8,16]{1,0:T(8,128)}, bf16[2048,1024]{1,0:T(8,128)(2,1)}, s32[64,8]{0,1:T(8,128)}, bf16[3,256,256]{2,1,0:T(8,128)(2,1)S(1)}, bf16[3,256,256]{2,1,0:T(8,128)(2,1)S(1)}, /*index=5*/bf16[3,256,256]{2,1,0:T(8,128)(2,1)}, bf16[3,256,256]{2,1,0:T(8,128)(2,1)}, ...), branch_computations={%region_0.1_spmd, %region_1.2_spmd} | conditional | flops 536870976 | bytes 55450716 | solution.py:549
  3.7 2.6 %collective-permute-start.1 = (bf16[3,256,256]{2,1,0:T(8,128)(2,1)S(1)}, bf16[3,256,256]{2,1,0:T(8,128)(2,1)S(1)}, u32[]{:S(2)}, u32[]{:S(2)}) collective-permute-start(bf16[3,256,256]{2,1,0:T(8,128)(2,1)S(1)} %get-tuple-element.51), channel_id=1, source_target_pairs={{0,4},{4,8},{8,12},{12,14},{14,10},{10,6},{6,2},{2,0},{1,5},{5,9},... | collective-permute-start | bytes 1179656 | tf_op jit(solution)/shard_map/cond/branch_0_fun/ppermute | solution.py:522
  6.4 2.0 %collective-permute-start.2 = (bf16[3,256,256]{2,1,0:T(8,128)(2,1)S(1)}, bf16[3,256,256]{2,1,0:T(8,128)(2,1)S(1)}, u32[]{:S(2)}, u32[]{:S(2)}) collective-permute-start(bf16[3,256,256]{2,1,0:T(8,128)(2,1)S(1)} %get-tuple-element.52), channel_id=1, source_target_pairs={{0,4},{4,8},{8,12},{12,14},{14,10},{10,6},{6,2},{2,0},{1,5},{5,9},... | collective-permute-start | bytes 1179656 | tf_op jit(solution)/shard_map/cond/branch_0_fun/ppermute | solution.py:522
  8.4 0.8 copy.14.a_mask
  10.0 0.9 %collective-permute-done.other_ref = bf16[2048,1024]{1,0:T(8,128)(2,1)} collective-permute-done((bf16[2048,1024]{1,0:T(8,128)(2,1)}, bf16[2048,1024]{1,0:T(8,128)(2,1)}, u32[]{:S(2)}, u32[]{:S(2)}) %collective-permute-start) | collective-permute-done | bytes 4194336 | tf_op jit(solution)/shard_map/cond/branch_0_fun/ppermute | solution.py:524
  10.9 5.6 %branch_0_fun.12.refs_0_ = bf16[8,2048,256]{2,1,0:T(8,128)(2,1)S(1)} custom-call(s32[18]{0:T(128)S(1)} %pad_add_fusion.place, s32[64,8]{1,0:T(8,128)S(1)} %copy.14.a_mask, bf16[2048,1024]{1,0:T(8,128)(2,1)} %get-tuple-element.49.own_ref, bf16[2048,1024]{1,0:T(8,128)(2,1)} %collective-permute-done.other_ref), custom_call_target="tpu_custom_call" | custom-call | bytes 131072 | tf_op jit(solution)/shard_map/cond/branch_0_fun/pallas_call | solution.py:44
  16.5 2.1 %collective-permute-done.3.refs_2_.refs_3_.refs_4_ = bf16[3,256,256]{2,1,0:T(8,128)(2,1)S(1)} collective-permute-done((bf16[3,256,256]{2,1,0:T(8,128)(2,1)}, bf16[3,256,256]{2,1,0:T(8,128)(2,1)S(1)}, u32[]{:S(2)}, u32[]{:S(2)}) %collective-permute-start.3) | collective-permute-done | bytes 393248 | tf_op jit(solution)/shard_map/cond/branch_0_fun/ppermute | solution.py:522
  19.2 1.6 %collective-permute-start.6 = (bf16[3,256,256]{2,1,0:T(8,128)(2,1)S(1)}, bf16[3,256,256]{2,1,0:T(8,128)(2,1)S(1)}, u32[]{:S(2)}, u32[]{:S(2)}) collective-permute-start(bf16[3,256,256]{2,1,0:T(8,128)(2,1)S(1)} %get-tuple-element.62), channel_id=1, source_target_pairs={{0,4},{4,8},{8,12},{12,14},{14,10},{10,6},{6,2},{2,0},{1,5},{5,9},... | collective-permute-start | bytes 1179656 | tf_op jit(solution)/shard_map/cond/branch_0_fun/ppermute | solution.py:522
  21.3 3.4 %collective-permute-done.2.refs_1_.refs_0_.refs_2_ = bf16[3,256,256]{2,1,0:T(8,128)(2,1)S(1)} collective-permute-done((bf16[3,256,256]{2,1,0:T(8,128)(2,1)S(1)}, bf16[3,256,256]{2,1,0:T(8,128)(2,1)S(1)}, u32[]{:S(2)}, u32[]{:S(2)}) %collective-permute-start.2) | collective-permute-done | bytes 393248 | tf_op jit(solution)/shard_map/cond/branch_0_fun/ppermute | solution.py:522
  24.7 2.3 %collective-permute-done.4.refs_3_.refs_2_.refs_5_ = bf16[3,256,256]{2,1,0:T(8,128)(2,1)S(1)} collective-permute-done((bf16[3,256,256]{2,1,0:T(8,128)(2,1)}, bf16[3,256,256]{2,1,0:T(8,128)(2,1)S(1)}, u32[]{:S(2)}, u32[]{:S(2)}) %collective-permute-start.4) | collective-permute-done | bytes 393248 | tf_op jit(solution)/shard_map/cond/branch_0_fun/ppermute | solution.py:522
  27.6 1.6 %collective-permute-start.5 = (bf16[3,256,256]{2,1,0:T(8,128)(2,1)S(1)}, bf16[3,256,256]{2,1,0:T(8,128)(2,1)S(1)}, u32[]{:S(2)}, u32[]{:S(2)}) collective-permute-start(bf16[3,256,256]{2,1,0:T(8,128)(2,1)S(1)} %get-tuple-element.55), channel_id=1, source_target_pairs={{0,4},{4,8},{8,12},{12,14},{14,10},{10,6},{6,2},{2,0},{1,5},{5,9},... | collective-permute-start | bytes 1179656 | tf_op jit(solution)/shard_map/cond/branch_0_fun/ppermute | solution.py:522
  29.7 6.2 %branch_0_fun.15.refs_7_ = f32[2048,2048]{1,0:T(8,128)S(1)} custom-call(s32[18]{0:T(128)S(1)} %pad_add_fusion.place, s32[8,16]{1,0:T(8,128)S(1)} %copy-done.2, bf16[8,2048,256]{2,1,0:T(8,128)(2,1)S(1)} %branch_0_fun.12.refs_0_, bf16[256,2048]{1,0:T(8,128)(2,1)S(1)} %copy-done, bf16[2048,2048]{1,0:T(8,128)(2,1)} %get-tuple-element.65.refs_2_), custom_call_target="tpu_custom_call" | custom-call | flops 33554432 | bytes 131072 | tf_op jit(solution)/shard_map/cond/branch_0_fun/pallas_call | solution.py:447
  36.7 2.0 %collective-permute-start.8 = (bf16[3,256,256]{2,1,0:T(8,128)(2,1)S(1)}, bf16[3,256,256]{2,1,0:T(8,128)(2,1)S(1)}, u32[]{:S(2)}, u32[]{:S(2)}) collective-permute-start(bf16[3,256,256]{2,1,0:T(8,128)(2,1)S(1)} %get-tuple-element.70), channel_id=1, source_target_pairs={{0,4},{4,8},{8,12},{12,14},{14,10},{10,6},{6,2},{2,0},{1,5},{5,9},... | collective-permute-start | bytes 1179656 | tf_op jit(solution)/shard_map/cond/branch_0_fun/ppermute | solution.py:522
  38.7 7.8 %branch_0_fun.18.refs_7_ = f32[2048,2048]{1,0:T(8,128)S(1)} custom-call(s32[18]{0:T(128)S(1)} %pad_add_fusion.place, s32[8,16]{1,0:T(8,128)S(1)} %copy-done.2, bf16[8,2048,256]{2,1,0:T(8,128)(2,1)S(1)} %branch_0_fun.12.refs_0_, bf16[3,256,256]{2,1,0:T(8,128)(2,1)S(1)} %collective-permute-done.1.refs_0_.refs_1_, ...), custom_call_target="tpu_custom_call", output_to_operand_aliasing={{}: (9, {})} | custom-call | flops 33554432 | bytes 131072 | tf_op jit(solution)/shard_map/cond/branch_0_fun/pallas_call | solution.py:447
  47.1 1.6 %collective-permute-start.12 = (bf16[3,256,256]{2,1,0:T(8,128)(2,1)S(1)}, bf16[3,256,256]{2,1,0:T(8,128)(2,1)S(1)}, u32[]{:S(2)}, u32[]{:S(2)}) collective-permute-start(bf16[3,256,256]{2,1,0:T(8,128)(2,1)S(1)} %get-tuple-element.78), channel_id=1, source_target_pairs={{0,4},{4,8},{8,12},{12,14},{14,10},{10,6},{6,2},{2,0},{1,5},{5,9},... | collective-permute-start | bytes 1179656 | tf_op jit(solution)/shard_map/cond/branch_0_fun/ppermute | solution.py:522
  49.2 3.1 %collective-permute-done.10.refs_3_.refs_6_.refs_2_.refs_4_ = bf16[3,256,256]{2,1,0:T(8,128)(2,1)S(1)} collective-permute-done((bf16[3,256,256]{2,1,0:T(8,128)(2,1)S(1)}, bf16[3,256,256]{2,1,0:T(8,128)(2,1)S(1)}, u32[]{:S(2)}, u32[]{:S(2)}) %collective-permute-start.10) | collective-permute-done | bytes 393248 | tf_op jit(solution)/shard_map/cond/branch_0_fun/ppermute | solution.py:522
  52.9 1.6 %collective-permute-start.11 = (bf16[3,256,256]{2,1,0:T(8,128)(2,1)S(1)}, bf16[3,256,256]{2,1,0:T(8,128)(2,1)S(1)}, u32[]{:S(2)}, u32[]{:S(2)}) collective-permute-start(bf16[3,256,256]{2,1,0:T(8,128)(2,1)S(1)} %get-tuple-element.73), channel_id=1, source_target_pairs={{0,4},{4,8},{8,12},{12,14},{14,10},{10,6},{6,2},{2,0},{1,5},{5,9},... | collective-permute-start | bytes 1179656 | tf_op jit(solution)/shard_map/cond/branch_0_fun/ppermute | solution.py:522
  55.0 7.8 %branch_0_fun.20.refs_7_ = f32[2048,2048]{1,0:T(8,128)S(1)} custom-call(s32[18]{0:T(128)S(1)} %pad_add_fusion.place, s32[8,16]{1,0:T(8,128)S(1)} %copy-done.2, bf16[8,2048,256]{2,1,0:T(8,128)(2,1)S(1)} %branch_0_fun.12.refs_0_, bf16[3,256,256]{2,1,0:T(8,128)(2,1)S(1)} %collective-permute-done.6.refs_1_.refs_3_.refs_0_, ...), custom_call_target="tpu_custom_call", output_to_operand_aliasing={{}: (9, {})} | custom-call | flops 33554432 | bytes 131072 | tf_op jit(solution)/shard_map/cond/branch_0_fun/pallas_call | solution.py:447
  63.5 1.6 %collective-permute-start.14 = (bf16[3,256,256]{2,1,0:T(8,128)(2,1)S(1)}, bf16[3,256,256]{2,1,0:T(8,128)(2,1)S(1)}, u32[]{:S(2)}, u32[]{:S(2)}) collective-permute-start(bf16[3,256,256]{2,1,0:T(8,128)(2,1)S(1)} %get-tuple-element.84), channel_id=1, source_target_pairs={{0,4},{4,8},{8,12},{12,14},{14,10},{10,6},{6,2},{2,0},{1,5},{5,9},... | collective-permute-start | bytes 1179656 | tf_op jit(solution)/shard_map/cond/branch_0_fun/ppermute | solution.py:522
  65.6 2.1 %collective-permute-done.11.refs_3_.refs_1_ = bf16[3,256,256]{2,1,0:T(8,128)(2,1)S(1)} collective-permute-done((bf16[3,256,256]{2,1,0:T(8,128)(2,1)S(1)}, bf16[3,256,256]{2,1,0:T(8,128)(2,1)S(1)}, u32[]{:S(2)}, u32[]{:S(2)}) %collective-permute-start.11) | collective-permute-done | bytes 393248 | tf_op jit(solution)/shard_map/cond/branch_0_fun/ppermute | solution.py:522
  67.6 1.6 %collective-permute-done.15.refs_6_.refs_3_ = bf16[3,256,256]{2,1,0:T(8,128)(2,1)S(1)} collective-permute-done((bf16[3,256,256]{2,1,0:T(8,128)(2,1)S(1)}, bf16[3,256,256]{2,1,0:T(8,128)(2,1)S(1)}, u32[]{:S(2)}, u32[]{:S(2)}) %collective-permute-start.15) | collective-permute-done | bytes 393248 | tf_op jit(solution)/shard_map/cond/branch_0_fun/ppermute | solution.py:522
  69.2 8.2 %branch_0_fun.22.refs_5_ = f32[2048,2048]{1,0:T(8,128)S(1)} custom-call(s32[18]{0:T(128)S(1)} %pad_add_fusion.place, s32[8,16]{1,0:T(8,128)S(1)} %copy-done.2, bf16[8,2048,256]{2,1,0:T(8,128)(2,1)S(1)} %branch_0_fun.12.refs_0_, bf16[3,256,256]{2,1,0:T(8,128)(2,1)S(1)} %collective-permute-done.8.refs_1_.refs_3_.refs_0_, ...), custom_call_target="tpu_custom_call", output_to_operand_aliasing={{}: (9, {})} | custom-call | flops 33554432 | bytes 131072 | tf_op jit(solution)/shard_map/cond/branch_0_fun/pallas_call | solution.py:447
  77.4 6.3 %branch_0_fun.23 = bf16[2048,2048]{1,0:T(8,128)(2,1)} custom-call(s32[18]{0:T(128)S(1)} %pad_add_fusion.place, s32[8,16]{1,0:T(8,128)S(1)} %copy-done.2, bf16[8,2048,256]{2,1,0:T(8,128)(2,1)S(1)} %branch_0_fun.12.refs_0_, bf16[3,256,256]{2,1,0:T(8,128)(2,1)S(1)} %collective-permute-done.11.refs_3_.refs_1_, ...), custom_call_target="tpu_custom_call" | custom-call | flops 33554432 | bytes 131072 | tf_op jit(solution)/shard_map/cond/branch_0_fun/pallas_call | solution.py:447
  (31 shorter events, 7.5 us)
Async XLA Ops:
  3.2 7.6 %collective-permute-start = (bf16[2048,1024]{1,0:T(8,128)(2,1)}, bf16[2048,1024]{1,0:T(8,128)(2,1)}, u32[]{:S(2)}, u32[]{:S(2)}) collective-permute-start(bf16[2048,1024]{1,0:T(8,128)(2,1)} %get-tuple-element.49.own_ref), channel_id=1, source_target_pairs={{0,1},{1,0},{2,3},{3,2},{4,5},{5,4},{6,7},{7,6},{8,9},{9,8},{10,11... | collective-permute-start | bytes 12582920 | tf_op jit(solution)/shard_map/cond/branch_0_fun/ppermute | solution.py:524
  3.7 12.7 %collective-permute-start.1 = (bf16[3,256,256]{2,1,0:T(8,128)(2,1)S(1)}, bf16[3,256,256]{2,1,0:T(8,128)(2,1)S(1)}, u32[]{:S(2)}, u32[]{:S(2)}) collective-permute-start(bf16[3,256,256]{2,1,0:T(8,128)(2,1)S(1)} %get-tuple-element.51), channel_id=1, source_target_pairs={{0,4},{4,8},{8,12},{12,14},{14,10},{10,6},{6,2},{2,0},{1,5},{5,9},... | collective-permute-start | bytes 1179656 | tf_op jit(solution)/shard_map/cond/branch_0_fun/ppermute | solution.py:522
  6.4 12.2 %collective-permute-start.3 = (bf16[3,256,256]{2,1,0:T(8,128)(2,1)}, bf16[3,256,256]{2,1,0:T(8,128)(2,1)S(1)}, u32[]{:S(2)}, u32[]{:S(2)}) collective-permute-start(bf16[3,256,256]{2,1,0:T(8,128)(2,1)} %get-tuple-element.53), channel_id=1, source_target_pairs={{4,0},{8,4},{12,8},{14,12},{10,14},{6,10},{2,6},{0,2},{5,1},{9,5},... | collective-permute-start | bytes 1179656 | tf_op jit(solution)/shard_map/cond/branch_0_fun/ppermute | solution.py:522
  6.4 18.3 %collective-permute-start.2 = (bf16[3,256,256]{2,1,0:T(8,128)(2,1)S(1)}, bf16[3,256,256]{2,1,0:T(8,128)(2,1)S(1)}, u32[]{:S(2)}, u32[]{:S(2)}) collective-permute-start(bf16[3,256,256]{2,1,0:T(8,128)(2,1)S(1)} %get-tuple-element.52), channel_id=1, source_target_pairs={{0,4},{4,8},{8,12},{12,14},{14,10},{10,6},{6,2},{2,0},{1,5},{5,9},... | collective-permute-start | bytes 1179656 | tf_op jit(solution)/shard_map/cond/branch_0_fun/ppermute | solution.py:522
  8.4 18.6 %collective-permute-start.4 = (bf16[3,256,256]{2,1,0:T(8,128)(2,1)}, bf16[3,256,256]{2,1,0:T(8,128)(2,1)S(1)}, u32[]{:S(2)}, u32[]{:S(2)}) collective-permute-start(bf16[3,256,256]{2,1,0:T(8,128)(2,1)} %get-tuple-element.54), channel_id=1, source_target_pairs={{4,0},{8,4},{12,8},{14,12},{10,14},{6,10},{2,6},{0,2},{5,1},{9,5},... | collective-permute-start | bytes 1179656 | tf_op jit(solution)/shard_map/cond/branch_0_fun/ppermute | solution.py:522
  10.0 19.7 %copy-start = (bf16[256,2048]{1,0:T(8,128)(2,1)S(1)}, bf16[256,2048]{1,0:T(8,128)(2,1)}, u32[]{:S(2)}) copy-start(bf16[256,2048]{1,0:T(8,128)(2,1)} %get-tuple-element.64.refs_1_) | copy-start | bytes 3145732 | tf_op jit(solution)/shard_map/cond
  10.0 19.7 %copy-start.2 = (s32[8,16]{1,0:T(8,128)S(1)}, s32[8,16]{1,0:T(8,128)}, u32[]{:S(2)}) copy-start(s32[8,16]{1,0:T(8,128)} %get-tuple-element.47.b_mask) | copy-start | bytes 1540 | tf_op jit(solution)/shard_map/cond
  19.2 16.8 %collective-permute-start.6 = (bf16[3,256,256]{2,1,0:T(8,128)(2,1)S(1)}, bf16[3,256,256]{2,1,0:T(8,128)(2,1)S(1)}, u32[]{:S(2)}, u32[]{:S(2)}) collective-permute-start(bf16[3,256,256]{2,1,0:T(8,128)(2,1)S(1)} %get-tuple-element.62), channel_id=1, source_target_pairs={{0,4},{4,8},{8,12},{12,14},{14,10},{10,6},{6,2},{2,0},{1,5},{5,9},... | collective-permute-start | bytes 1179656 | tf_op jit(solution)/shard_map/cond/branch_0_fun/ppermute | solution.py:522
  20.8 15.2 %collective-permute-start.7 = (bf16[3,256,256]{2,1,0:T(8,128)(2,1)S(1)}, bf16[3,256,256]{2,1,0:T(8,128)(2,1)S(1)}, u32[]{:S(2)}, u32[]{:S(2)}) collective-permute-start(bf16[3,256,256]{2,1,0:T(8,128)(2,1)S(1)} %get-tuple-element.63), channel_id=1, source_target_pairs={{4,0},{8,4},{12,8},{14,12},{10,14},{6,10},{2,6},{0,2},{5,1},{9,5},... | collective-permute-start | bytes 1179656 | tf_op jit(solution)/shard_map/cond/branch_0_fun/ppermute | solution.py:522
  27.6 18.8 %collective-permute-start.5 = (bf16[3,256,256]{2,1,0:T(8,128)(2,1)S(1)}, bf16[3,256,256]{2,1,0:T(8,128)(2,1)S(1)}, u32[]{:S(2)}, u32[]{:S(2)}) collective-permute-start(bf16[3,256,256]{2,1,0:T(8,128)(2,1)S(1)} %get-tuple-element.55), channel_id=1, source_target_pairs={{0,4},{4,8},{8,12},{12,14},{14,10},{10,6},{6,2},{2,0},{1,5},{5,9},... | collective-permute-start | bytes 1179656 | tf_op jit(solution)/shard_map/cond/branch_0_fun/ppermute | solution.py:522
  29.2 17.2 %collective-permute-start.9 = (bf16[3,256,256]{2,1,0:T(8,128)(2,1)S(1)}, bf16[3,256,256]{2,1,0:T(8,128)(2,1)S(1)}, u32[]{:S(2)}, u32[]{:S(2)}) collective-permute-start(bf16[3,256,256]{2,1,0:T(8,128)(2,1)S(1)} %get-tuple-element.71), channel_id=1, source_target_pairs={{4,0},{8,4},{12,8},{14,12},{10,14},{6,10},{2,6},{0,2},{5,1},{9,5},... | collective-permute-start | bytes 1179656 | tf_op jit(solution)/shard_map/cond/branch_0_fun/ppermute | solution.py:522
  36.6 15.6 %collective-permute-start.10 = (bf16[3,256,256]{2,1,0:T(8,128)(2,1)S(1)}, bf16[3,256,256]{2,1,0:T(8,128)(2,1)S(1)}, u32[]{:S(2)}, u32[]{:S(2)}) collective-permute-start(bf16[3,256,256]{2,1,0:T(8,128)(2,1)S(1)} %get-tuple-element.72), channel_id=1, source_target_pairs={{4,0},{8,4},{12,8},{14,12},{10,14},{6,10},{2,6},{0,2},{5,1},{9,5},... | collective-permute-start | bytes 1179656 | tf_op jit(solution)/shard_map/cond/branch_0_fun/ppermute | solution.py:522
  36.7 15.6 %collective-permute-start.8 = (bf16[3,256,256]{2,1,0:T(8,128)(2,1)S(1)}, bf16[3,256,256]{2,1,0:T(8,128)(2,1)S(1)}, u32[]{:S(2)}, u32[]{:S(2)}) collective-permute-start(bf16[3,256,256]{2,1,0:T(8,128)(2,1)S(1)} %get-tuple-element.70), channel_id=1, source_target_pairs={{0,4},{4,8},{8,12},{12,14},{14,10},{10,6},{6,2},{2,0},{1,5},{5,9},... | collective-permute-start | bytes 1179656 | tf_op jit(solution)/shard_map/cond/branch_0_fun/ppermute | solution.py:522
  47.1 15.7 %collective-permute-start.12 = (bf16[3,256,256]{2,1,0:T(8,128)(2,1)S(1)}, bf16[3,256,256]{2,1,0:T(8,128)(2,1)S(1)}, u32[]{:S(2)}, u32[]{:S(2)}) collective-permute-start(bf16[3,256,256]{2,1,0:T(8,128)(2,1)S(1)} %get-tuple-element.78), channel_id=1, source_target_pairs={{0,4},{4,8},{8,12},{12,14},{14,10},{10,6},{6,2},{2,0},{1,5},{5,9},... | collective-permute-start | bytes 1179656 | tf_op jit(solution)/shard_map/cond/branch_0_fun/ppermute | solution.py:522
  48.7 14.1 %collective-permute-start.13 = (bf16[3,256,256]{2,1,0:T(8,128)(2,1)S(1)}, bf16[3,256,256]{2,1,0:T(8,128)(2,1)S(1)}, u32[]{:S(2)}, u32[]{:S(2)}) collective-permute-start(bf16[3,256,256]{2,1,0:T(8,128)(2,1)S(1)} %get-tuple-element.79), channel_id=1, source_target_pairs={{4,0},{8,4},{12,8},{14,12},{10,14},{6,10},{2,6},{0,2},{5,1},{9,5},... | collective-permute-start | bytes 1179656 | tf_op jit(solution)/shard_map/cond/branch_0_fun/ppermute | solution.py:522
  52.9 14.7 %collective-permute-start.11 = (bf16[3,256,256]{2,1,0:T(8,128)(2,1)S(1)}, bf16[3,256,256]{2,1,0:T(8,128)(2,1)S(1)}, u32[]{:S(2)}, u32[]{:S(2)}) collective-permute-start(bf16[3,256,256]{2,1,0:T(8,128)(2,1)S(1)} %get-tuple-element.73), channel_id=1, source_target_pairs={{0,4},{4,8},{8,12},{12,14},{14,10},{10,6},{6,2},{2,0},{1,5},{5,9},... | collective-permute-start | bytes 1179656 | tf_op jit(solution)/shard_map/cond/branch_0_fun/ppermute | solution.py:522
  54.5 14.7 %collective-permute-start.15 = (bf16[3,256,256]{2,1,0:T(8,128)(2,1)S(1)}, bf16[3,256,256]{2,1,0:T(8,128)(2,1)S(1)}, u32[]{:S(2)}, u32[]{:S(2)}) collective-permute-start(bf16[3,256,256]{2,1,0:T(8,128)(2,1)S(1)} %get-tuple-element.85), channel_id=1, source_target_pairs={{4,0},{8,4},{12,8},{14,12},{10,14},{6,10},{2,6},{0,2},{5,1},{9,5},... | collective-permute-start | bytes 1179656 | tf_op jit(solution)/shard_map/cond/branch_0_fun/ppermute | solution.py:522
  63.5 13.9 %collective-permute-start.14 = (bf16[3,256,256]{2,1,0:T(8,128)(2,1)S(1)}, bf16[3,256,256]{2,1,0:T(8,128)(2,1)S(1)}, u32[]{:S(2)}, u32[]{:S(2)}) collective-permute-start(bf16[3,256,256]{2,1,0:T(8,128)(2,1)S(1)} %get-tuple-element.84), channel_id=1, source_target_pairs={{0,4},{4,8},{8,12},{12,14},{14,10},{10,6},{6,2},{2,0},{1,5},{5,9},... | collective-permute-start | bytes 1179656 | tf_op jit(solution)/shard_map/cond/branch_0_fun/ppermute | solution.py:522
  65.1 12.3 %collective-permute-start.16 = (bf16[3,256,256]{2,1,0:T(8,128)(2,1)S(1)}, bf16[3,256,256]{2,1,0:T(8,128)(2,1)S(1)}, u32[]{:S(2)}, u32[]{:S(2)}) collective-permute-start(bf16[3,256,256]{2,1,0:T(8,128)(2,1)S(1)} %get-tuple-element.86), channel_id=1, source_target_pairs={{4,0},{8,4},{12,8},{14,12},{10,14},{6,10},{2,6},{0,2},{5,1},{9,5},... | collective-permute-start | bytes 1179656 | tf_op jit(solution)/shard_map/cond/branch_0_fun/ppermute | solution.py:522

commit v4 on v3

--- a/solution.py
+++ b/solution.py
@@ -219,66 +219,76 @@
     return out
 
 
-def pack_body(b_mask, b_hbm, *refs, n, tiles):
-    plan = refs[6]
-    rows, (b_ref, arrived) = refs[7:9], refs[9:]
-    ring = ring_of(n)
+def pack_body(b_mask, b_ref, *refs, n, tiles, head):
     depth = b_ref.shape[0]
-    fetch = pltpu.make_async_copy(b_hbm, b_ref, arrived)
-    fetch.start()
-    far = n // 2
-    need = jnp.int32(0)
-    for c in range(2):
-        kept = []
-        for owner in ring:
-            total = jnp.int32(0)
-            for j in range(tiles):
-                total += b_mask[owner * depth // TW, c * tiles + j]
-            kept.append(total)
-        span = [jnp.maximum(total, 2 * SEND) for total in kept]
-        for q in range(n):
-            right = sum(span[(q - hop) % n] for hop in range(1, far))
-            left = sum(span[(q + hop) % n] for hop in range(1, far))
-            both = lax.shift_right_logical(right + left + kept[(q + far) % n] + 1, 1)
-            need = jnp.maximum(need, jnp.maximum(jnp.maximum(right, left), both))
-    plan[0] = need
-
+    arrived = refs[-1]
     mine = lax.axis_index("row") * depth // TW
     half = lax.axis_index("col") * tiles
     flags = [b_mask[mine, half + j] for j in range(tiles)]
     total = sum(flags)
+    end = jnp.maximum(total, 2 * SEND)
+
+    def put(ref, low, j, at):
+        @pl.when((at >= low) & (at < low + SEND))
+        def _():
+            pltpu.make_async_copy(b_ref.at[:, j * TW : (j + 1) * TW], ref.at[at - low], arrived).start()
+
     before = jnp.int32(0)
-    fetch.wait()
     for j in range(tiles):
-        tile = b_ref[:, j * TW : (j + 1) * TW]
         dropped = total + j - before
-        rows[0][jnp.where(flags[j] != 0, before, dropped)] = tile
-        rows[1][jnp.where(flags[j] != 0, total - 1 - before, dropped)] = tile
+        places = (jnp.where(flags[j] != 0, before, dropped), jnp.where(flags[j] != 0, total - 1 - before, dropped))
+        for side, at in enumerate(places):
+            if head:
+                put(refs[side], 0, j, at)
+            else:
+                put(refs[2 * side], SEND, j, at)
+                put(refs[2 * side + 1], end - SEND, j, at)
         before += flags[j]
-    end = jnp.maximum(total, 2 * SEND)
-    plan[1] = 3 * SEND - end
-    for side in range(2):
-        refs[3 * side][...] = rows[side][:SEND]
-        refs[3 * side + 1][...] = rows[side][SEND : 2 * SEND]
-        for i in range(SEND):
-            refs[3 * side + 2][i] = rows[side][end - SEND + i]
-
-
-def pack(b_mask, b_tiles, n):
+
+    if head:
+        plan = refs[2]
+        ring = ring_of(n)
+        far = n // 2
+        need = jnp.int32(0)
+        for c in range(2):
+            kept = []
+            for owner in ring:
+                count = jnp.int32(0)
+                for j in range(tiles):
+                    count += b_mask[owner * depth // TW, c * tiles + j]
+                kept.append(count)
+            span = [jnp.maximum(count, 2 * SEND) for count in kept]
+            for q in range(n):
+                right = sum(span[(q - hop) % n] for hop in range(1, far))
+                left = sum(span[(q + hop) % n] for hop in range(1, far))
+                both = lax.shift_right_logical(right + left + kept[(q + far) % n] + 1, 1)
+                need = jnp.maximum(need, jnp.maximum(jnp.maximum(right, left), both))
+        plan[0] = need
+        plan[1] = 3 * SEND - end
+    for ref in refs[: 2 if head else 4]:
+        pltpu.make_async_copy(ref, ref, arrived).wait()
+
+
+def pack(b_mask, b_tiles, n, head):
     depth, width = b_tiles.shape
-    tiles = width // TW
     whole = pl.BlockSpec(memory_space=pltpu.VMEM)
+    count = 2 if head else 4
+    out_shape = [pltpu.VMEM((SEND, depth, TW), jnp.bfloat16)] * count
+    out_specs = [whole] * count
+    if head:
+        out_shape.append(jax.ShapeDtypeStruct((2,), jnp.int32))
+        out_specs.append(pl.BlockSpec(memory_space=pltpu.SMEM))
     return pl.pallas_call(
-        functools.partial(pack_body, n=n, tiles=tiles),
+        functools.partial(pack_body, n=n, tiles=width // TW, head=head),
         grid_spec=pltpu.PrefetchScalarGridSpec(
             num_scalar_prefetch=1,
             grid=(1,),
             in_specs=[pl.BlockSpec(memory_space=pl.ANY)],
-            out_specs=[whole] * 6 + [pl.BlockSpec(memory_space=pltpu.SMEM)],
-            scratch_shapes=[pltpu.VMEM((tiles, depth, TW), jnp.bfloat16)] * 2
-            + [pltpu.VMEM((depth, width), jnp.bfloat16), pltpu.SemaphoreType.DMA],
-        ),
-        out_shape=[pltpu.VMEM((SEND, depth, TW), jnp.bfloat16)] * 6 + [jax.ShapeDtypeStruct((2,), jnp.int32)],
+            out_specs=out_specs,
+            scratch_shapes=[pltpu.SemaphoreType.DMA],
+        ),
+        out_shape=out_shape,
+        cost_estimate=pl.CostEstimate(flops=0, bytes_accessed=1024, transcendentals=0),
         compiler_params=pltpu.CompilerParams(vmem_limit_bytes=VMEM),
     )(b_mask, pltpu.with_memory_space_constraint(b_tiles, pltpu.HBM))
 
@@ -345,6 +355,7 @@
             firsts[offset] = sum(flags[:wide])
             totals[offset] = firsts[offset] + sum(flags[wide:])
         waiting = jnp.int32(0)
+        leftover = []
         for slot in range(start, high):
             rows = slice((slot - start) * depth, (slot - start + 1) * depth)
             offset = offsets[slot]
@@ -375,15 +386,24 @@
                 else:
                     side = 0 if offset < 0 else 1
                     valid = flag
+                    index = jnp.clip(at[side] - begin, 0, stores[side].shape[0] - 1)
                     if slot < low:
                         valid = jnp.where(at[side] >= carried, flag, 0)
                         waiting += valid
-                    elif limit is not None:
-                        valid = jnp.where(at[side] < limit, flag, 0)
-                    index = jnp.clip(at[side] - begin, 0, stores[side].shape[0] - 1)
-                    kept[rows, columns] = stores[side][index] * valid.astype(kept.dtype)
+                        leftover.append((rows, columns, side, index, valid))
+                    else:
+                        if limit is not None:
+                            valid = jnp.where(at[side] < limit, flag, 0)
+                        kept[rows, columns] = stores[side][index] * valid.astype(kept.dtype)
                 before += flag
         late[0] = waiting
+        if carry:
+
+            @pl.when(waiting != 0)
+            def _():
+                for rows, columns, side, index, valid in leftover:
+                    kept[rows, columns] = stores[side][index] * valid.astype(kept.dtype)
+
 
     height = a_ref.shape[1]
     row_count = height // STEPS_OF[final]
@@ -465,7 +485,7 @@
     )(*operands)
 
 
-def sparse(n, cap, a_tiles, b_tiles, a_mask, b_mask, c_given, plan, *packed):
+def sparse(n, cap, a_tiles, b_tiles, a_mask, b_mask, c_given, plan, *heads):
     ring = ring_of(n)
     right = [(ring[i], ring[(i + 1) % n]) for i in range(n)]
     left = [(t, s) for s, t in right]
@@ -484,18 +504,18 @@
     cut = 1 + 2 * ((far - 1) // 2)
     near, edge = 2 * far - 3, 2 * far - 1
     middle = (sent_by(tiles * (far - 2)) - 1) * SEND
-    limit = (last - 1) * SEND
+    limit = (cap - 2) // SEND * SEND
     phases = [
         dict(low=0, high=1, carry=0, carried=0, limit=None, sends_of=()),
         dict(low=1, high=cut, carry=0, carried=0, limit=None, sends_of=(0, sent_by(tiles * (cut // 2)))),
         dict(low=cut, high=near, carry=0, carried=0, limit=middle, sends_of=(2 * (cut // 2), middle // SEND)),
         dict(
             low=near, high=edge, carry=near - cut, carried=middle, limit=limit,
-            sends_of=(min(2 * (far - 2), middle // SEND), last - 1),
+            sends_of=(min(2 * (far - 2), middle // SEND), limit // SEND),
         ),
         dict(
             low=edge, high=n, carry=edge - near, carried=limit, limit=None,
-            sends_of=(min(2 * (far - 1), last - 1), last),
+            sends_of=(min(2 * (far - 1), limit // SEND), last),
         ),
     ]
     work = collections.defaultdict(list)
@@ -509,12 +529,15 @@
     other = a_kept = total = None
     for index in range(last + 1):
         if index < last:
-            if index < 2:
-                sources = [packed[index], packed[3 + index]]
+            if index == 0:
+                sources = heads
+            elif index == 1:
+                packed = pack(b_mask, b_tiles, n, False)
+                sources = packed[::2]
             else:
                 arrays = []
                 for side in range(2):
-                    arrays += [packed[3 * side + 2] if index == 2 else sends[index - 3][side], sends[index - 2][side]]
+                    arrays += [packed[2 * side + 1] if index == 2 else sends[index - 3][side], sends[index - 2][side]]
                 if tied:
                     *arrays, _ = lax.optimization_barrier((*arrays, tied))
                     tied = []
@@ -539,14 +562,14 @@
 
 def on_device(n, *args):
     b_tiles, b_mask = args[1], args[3]
-    *packed, plan = pack(b_mask, b_tiles, n)
+    *heads, plan = pack(b_mask, b_tiles, n, True)
     tiles = b_tiles.shape[1] // TW
     most = tiles * (n // 2 - 1) + tiles // 2
-    caps = [most - most * saved // 28 for saved in (4,)]
+    caps = [most - most * saved // 28 for saved in (4, 3)]
     branches = [functools.partial(sparse, n, cap) for cap in caps]
     branches.append(lambda *operands: dense(n, *operands[:5]))
     which = sum((plan[0] > cap).astype(jnp.int32) for cap in caps)
-    return lax.switch(which, branches, *args, plan, *packed)
+    return lax.switch(which, branches, *args, plan, *heads)
 
 
 def solution(mesh):

time: 84 us -> 82.8 us (0.986)
  waiting for transfers between devices: 15.4 us -> 11.9 us
  Pallas kernels: 48.9 us -> 51 us
    ppermute x16, waiting for transfers between devices: 14.5 us -> 11.9 us  [sparse(): lax.ppermute(source, 'row', pairs)]
    pallas_call x1 -> x2, Pallas kernels: 3.15 us -> 5.71 us  [pack(): pl.pallas_call(functools.partial(pack_body, n=n, tiles=width // TW, head=...]
    ppermute x1, waiting for transfers between devices: 0.89 us -> 0.01 us  [sparse(): other = lax.ppermute(a_tiles, 'col', [(0, 1), (1, 0)])]
  transfers between devices with their start and end apart: 17 -> 17, of which waited for: 7 -> 5; matrix products, arithmetic and copies ran while one was open for 2% -> 2% of each run, Pallas kernels for 47% -> 51%
where the time goes in v4:
time: 82.8 us; the launch traced here: 82.5 us
  Pallas kernels  51 us (62%)
  starting transfers between devices  17.8 us (21%)
  waiting for transfers between devices  11.9 us (14%)
  local copies, waits for them, and re-layouts  1.47 us (2%)
    pallas_call x5, Pallas kernels, gather_multiply(): pl.pallas_call(functools.partial(gather_multiply_body, low=low, high=high...  35.8 us
    ppermute x16, starting transfers between devices, sparse(): lax.ppermute(source, 'row', pairs)  17.3 us
    ppermute x16, waiting for transfers between devices, sparse(): lax.ppermute(source, 'row', pairs)  11.9 us
    pallas_call x2, Pallas kernels, pack(): pl.pallas_call(functools.partial(pack_body, n=n, tiles=width // TW, head=...  5.71 us
    pallas_call x1, Pallas kernels, prepare(): pl.pallas_call(functools.partial(prepare_body, depth=depth, n=n), grid_sp...  5.62 us
    pallas_call x6, Pallas kernels, choose(): pl.pallas_call(functools.partial(choose_body, count=count), grid_spec=plt...  3.79 us
  transfers between devices with their start and end apart: 17, of which 5 were waited for; matrix products, arithmetic and copies ran while one was open for 2% of the time, Pallas kernels for 51%

profile of v4, /device:TPU:0, one launch (start us, length us, event | category | flops | bytes accessed | tf_op | source)
XLA Modules:
  0.0 82.5 jit_solution(14690038012642348111)
XLA Ops:
  0.0 2.6 %shard_map.85 = (bf16[3,256,256]{2,1,0:T(8,128)(2,1)S(1)}, bf16[3,256,256]{2,1,0:T(8,128)(2,1)S(1)}, s32[2]{0:T(128)S(1)}) custom-call(s32[8,16]{1,0:T(8,128)} %b_mask.1, bf16[256,2048]{1,0:T(8,128)(2,1)} %b_ref.1), custom_call_target="tpu_custom_call" | custom-call | bytes 1024 | tf_op jit(solution)/shard_map/pallas_call | solution.py:281
  2.7 79.8 %conditional.1 = (bf16[2048,2048]{1,0:T(8,128)(2,1)}) conditional(s32[]{:T(128)} %bitcast.9, (s32[8,16]{1,0:T(8,128)}, bf16[2048,1024]{1,0:T(8,128)(2,1)}, s32[64,8]{0,1:T(8,128)}, bf16[3,256,256]{2,1,0:T(8,128)(2,1)S(1)}, s32[8,16]{1,0:T(8,128)}, /*index=5*/bf16[256,2048]{1,0:T(8,128)(2,1)}, bf16[3,256,256]{2,1,0:T(8,128)(2,1)S(1)}, ...), branch_computations={%region_0.1_spmd, %region_1.2_spmd, %region_2.3_spmd} | conditional | flops 536870976 | bytes 55450716 | solution.py:572
  3.2 2.6 %collective-permute-start.1 = (bf16[3,256,256]{2,1,0:T(8,128)(2,1)S(1)}, bf16[3,256,256]{2,1,0:T(8,128)(2,1)S(1)}, u32[]{:S(2)}, u32[]{:S(2)}) collective-permute-start(bf16[3,256,256]{2,1,0:T(8,128)(2,1)S(1)} %get-tuple-element.62), channel_id=1, source_target_pairs={{0,4},{4,8},{8,12},{12,14},{14,10},{10,6},{6,2},{2,0},{1,5},{5,9},... | collective-permute-start | bytes 1179656 | tf_op jit(solution)/shard_map/cond/branch_0_fun/ppermute | solution.py:545
  5.9 3.1 %branch_0_fun.14 = (bf16[3,256,256]{2,1,0:T(8,128)(2,1)}, bf16[3,256,256]{2,1,0:T(8,128)(2,1)S(1)}, bf16[3,256,256]{2,1,0:T(8,128)(2,1)}, bf16[3,256,256]{2,1,0:T(8,128)(2,1)S(1)}) custom-call(s32[8,16]{1,0:T(8,128)} %get-tuple-element.58.b_mask, bf16[256,2048]{1,0:T(8,128)(2,1)} %get-tuple-element.63.b_ref.refs_1_), custom_call_target="tpu_custom_call" | custom-call | bytes 1024 | tf_op jit(solution)/shard_map/cond/branch_0_fun/pallas_call | solution.py:281
  9.0 2.0 %collective-permute-start.2 = (bf16[3,256,256]{2,1,0:T(8,128)(2,1)}, bf16[3,256,256]{2,1,0:T(8,128)(2,1)S(1)}, u32[]{:S(2)}, u32[]{:S(2)}) collective-permute-start(bf16[3,256,256]{2,1,0:T(8,128)(2,1)} %get-tuple-element.64), channel_id=1, source_target_pairs={{0,4},{4,8},{8,12},{12,14},{14,10},{10,6},{6,2},{2,0},{1,5},{5,9},... | collective-permute-start | bytes 1179656 | tf_op jit(solution)/shard_map/cond/branch_0_fun/ppermute | solution.py:545
  11.2 0.8 copy.19.a_mask
  12.0 0.7 dynamic-slice_bitcast_fusion
  12.7 5.6 %branch_0_fun.13.refs_0_ = bf16[8,2048,256]{2,1,0:T(8,128)(2,1)S(1)} custom-call(s32[18]{0:T(128)S(1)} %pad_add_fusion.place, s32[64,8]{1,0:T(8,128)S(1)} %copy.19.a_mask, bf16[2048,1024]{1,0:T(8,128)(2,1)} %get-tuple-element.60.own_ref, bf16[2048,1024]{1,0:T(8,128)(2,1)} %collective-permute-done.other_ref), custom_call_target="tpu_custom_call" | custom-call | bytes 131072 | tf_op jit(solution)/shard_map/cond/branch_0_fun/pallas_call | solution.py:44
  19.0 1.9 %collective-permute-start.6 = (bf16[3,256,256]{2,1,0:T(8,128)(2,1)S(1)}, bf16[3,256,256]{2,1,0:T(8,128)(2,1)S(1)}, u32[]{:S(2)}, u32[]{:S(2)}) collective-permute-start(bf16[3,256,256]{2,1,0:T(8,128)(2,1)S(1)} %get-tuple-element.74), channel_id=1, source_target_pairs={{0,4},{4,8},{8,12},{12,14},{14,10},{10,6},{6,2},{2,0},{1,5},{5,9},... | collective-permute-start | bytes 1179656 | tf_op jit(solution)/shard_map/cond/branch_0_fun/ppermute | solution.py:545
  21.1 3.1 %collective-permute-done.2.refs_1_.refs_0_.refs_2_ = bf16[3,256,256]{2,1,0:T(8,128)(2,1)S(1)} collective-permute-done((bf16[3,256,256]{2,1,0:T(8,128)(2,1)}, bf16[3,256,256]{2,1,0:T(8,128)(2,1)S(1)}, u32[]{:S(2)}, u32[]{:S(2)}) %collective-permute-start.2) | collective-permute-done | bytes 393248 | tf_op jit(solution)/shard_map/cond/branch_0_fun/ppermute | solution.py:545
  24.2 2.0 %collective-permute-done.4.refs_3_.refs_2_.refs_5_ = bf16[3,256,256]{2,1,0:T(8,128)(2,1)S(1)} collective-permute-done((bf16[3,256,256]{2,1,0:T(8,128)(2,1)}, bf16[3,256,256]{2,1,0:T(8,128)(2,1)S(1)}, u32[]{:S(2)}, u32[]{:S(2)}) %collective-permute-start.4) | collective-permute-done | bytes 393248 | tf_op jit(solution)/shard_map/cond/branch_0_fun/ppermute | solution.py:545
  26.9 1.6 %collective-permute-start.5 = (bf16[3,256,256]{2,1,0:T(8,128)(2,1)S(1)}, bf16[3,256,256]{2,1,0:T(8,128)(2,1)S(1)}, u32[]{:S(2)}, u32[]{:S(2)}) collective-permute-start(bf16[3,256,256]{2,1,0:T(8,128)(2,1)S(1)} %get-tuple-element.67), channel_id=1, source_target_pairs={{0,4},{4,8},{8,12},{12,14},{14,10},{10,6},{6,2},{2,0},{1,5},{5,9},... | collective-permute-start | bytes 1179656 | tf_op jit(solution)/shard_map/cond/branch_0_fun/ppermute | solution.py:545
  28.9 6.3 %branch_0_fun.17.refs_7_ = f32[2048,2048]{1,0:T(8,128)S(1)} custom-call(s32[18]{0:T(128)S(1)} %pad_add_fusion.place, s32[8,16]{1,0:T(8,128)S(1)} %copy-done.3, bf16[8,2048,256]{2,1,0:T(8,128)(2,1)S(1)} %branch_0_fun.13.refs_0_, bf16[256,2048]{1,0:T(8,128)(2,1)S(1)} %copy-done, bf16[2048,2048]{1,0:T(8,128)(2,1)} %get-tuple-element.76.refs_2_), custom_call_target="tpu_custom_call" | custom-call | flops 33554432 | bytes 131072 | tf_op jit(solution)/shard_map/cond/branch_0_fun/pallas_call | solution.py:467
  35.9 2.0 %collective-permute-start.8 = (bf16[3,256,256]{2,1,0:T(8,128)(2,1)S(1)}, bf16[3,256,256]{2,1,0:T(8,128)(2,1)S(1)}, u32[]{:S(2)}, u32[]{:S(2)}) collective-permute-start(bf16[3,256,256]{2,1,0:T(8,128)(2,1)S(1)} %get-tuple-element.81), channel_id=1, source_target_pairs={{0,4},{4,8},{8,12},{12,14},{14,10},{10,6},{6,2},{2,0},{1,5},{5,9},... | collective-permute-start | bytes 1179656 | tf_op jit(solution)/shard_map/cond/branch_0_fun/ppermute | solution.py:545
  37.9 7.8 %branch_0_fun.20.refs_7_ = f32[2048,2048]{1,0:T(8,128)S(1)} custom-call(s32[18]{0:T(128)S(1)} %pad_add_fusion.place, s32[8,16]{1,0:T(8,128)S(1)} %copy-done.3, bf16[8,2048,256]{2,1,0:T(8,128)(2,1)S(1)} %branch_0_fun.13.refs_0_, bf16[3,256,256]{2,1,0:T(8,128)(2,1)S(1)} %collective-permute-done.1.refs_0_.refs_1_, ...), custom_call_target="tpu_custom_call", output_to_operand_aliasing={{}: (9, {})} | custom-call | flops 33554432 | bytes 131072 | tf_op jit(solution)/shard_map/cond/branch_0_fun/pallas_call | solution.py:467
  46.4 1.6 %collective-permute-start.12 = (bf16[3,256,256]{2,1,0:T(8,128)(2,1)S(1)}, bf16[3,256,256]{2,1,0:T(8,128)(2,1)S(1)}, u32[]{:S(2)}, u32[]{:S(2)}) collective-permute-start(bf16[3,256,256]{2,1,0:T(8,128)(2,1)S(1)} %get-tuple-element.89), channel_id=1, source_target_pairs={{0,4},{4,8},{8,12},{12,14},{14,10},{10,6},{6,2},{2,0},{1,5},{5,9},... | collective-permute-start | bytes 1179656 | tf_op jit(solution)/shard_map/cond/branch_0_fun/ppermute | solution.py:545
  48.4 3.1 %collective-permute-done.10.refs_3_.refs_6_.refs_2_.refs_4_ = bf16[3,256,256]{2,1,0:T(8,128)(2,1)S(1)} collective-permute-done((bf16[3,256,256]{2,1,0:T(8,128)(2,1)S(1)}, bf16[3,256,256]{2,1,0:T(8,128)(2,1)S(1)}, u32[]{:S(2)}, u32[]{:S(2)}) %collective-permute-start.10) | collective-permute-done | bytes 393248 | tf_op jit(solution)/shard_map/cond/branch_0_fun/ppermute | solution.py:545
  52.1 1.6 %collective-permute-start.11 = (bf16[3,256,256]{2,1,0:T(8,128)(2,1)S(1)}, bf16[3,256,256]{2,1,0:T(8,128)(2,1)S(1)}, u32[]{:S(2)}, u32[]{:S(2)}) collective-permute-start(bf16[3,256,256]{2,1,0:T(8,128)(2,1)S(1)} %get-tuple-element.84), channel_id=1, source_target_pairs={{0,4},{4,8},{8,12},{12,14},{14,10},{10,6},{6,2},{2,0},{1,5},{5,9},... | collective-permute-start | bytes 1179656 | tf_op jit(solution)/shard_map/cond/branch_0_fun/ppermute | solution.py:545
  54.2 7.8 %branch_0_fun.22.refs_7_ = f32[2048,2048]{1,0:T(8,128)S(1)} custom-call(s32[18]{0:T(128)S(1)} %pad_add_fusion.place, s32[8,16]{1,0:T(8,128)S(1)} %copy-done.3, bf16[8,2048,256]{2,1,0:T(8,128)(2,1)S(1)} %branch_0_fun.13.refs_0_, bf16[3,256,256]{2,1,0:T(8,128)(2,1)S(1)} %collective-permute-done.6.refs_1_.refs_3_.refs_0_, ...), custom_call_target="tpu_custom_call", output_to_operand_aliasing={{}: (9, {})} | custom-call | flops 33554432 | bytes 131072 | tf_op jit(solution)/shard_map/cond/branch_0_fun/pallas_call | solution.py:467
  62.7 1.6 %collective-permute-start.14 = (bf16[3,256,256]{2,1,0:T(8,128)(2,1)S(1)}, bf16[3,256,256]{2,1,0:T(8,128)(2,1)S(1)}, u32[]{:S(2)}, u32[]{:S(2)}) collective-permute-start(bf16[3,256,256]{2,1,0:T(8,128)(2,1)S(1)} %get-tuple-element.95), channel_id=1, source_target_pairs={{0,4},{4,8},{8,12},{12,14},{14,10},{10,6},{6,2},{2,0},{1,5},{5,9},... | collective-permute-start | bytes 1179656 | tf_op jit(solution)/shard_map/cond/branch_0_fun/ppermute | solution.py:545
  64.8 2.1 %collective-permute-done.11.refs_3_.refs_1_ = bf16[3,256,256]{2,1,0:T(8,128)(2,1)S(1)} collective-permute-done((bf16[3,256,256]{2,1,0:T(8,128)(2,1)S(1)}, bf16[3,256,256]{2,1,0:T(8,128)(2,1)S(1)}, u32[]{:S(2)}, u32[]{:S(2)}) %collective-permute-start.11) | collective-permute-done | bytes 393248 | tf_op jit(solution)/shard_map/cond/branch_0_fun/ppermute | solution.py:545
  66.9 1.6 %collective-permute-done.15.refs_6_.refs_3_ = bf16[3,256,256]{2,1,0:T(8,128)(2,1)S(1)} collective-permute-done((bf16[3,256,256]{2,1,0:T(8,128)(2,1)S(1)}, bf16[3,256,256]{2,1,0:T(8,128)(2,1)S(1)}, u32[]{:S(2)}, u32[]{:S(2)}) %collective-permute-start.15) | collective-permute-done | bytes 393248 | tf_op jit(solution)/shard_map/cond/branch_0_fun/ppermute | solution.py:545
  68.5 8.0 %branch_0_fun.24.refs_5_ = f32[2048,2048]{1,0:T(8,128)S(1)} custom-call(s32[18]{0:T(128)S(1)} %pad_add_fusion.place, s32[8,16]{1,0:T(8,128)S(1)} %copy-done.3, bf16[8,2048,256]{2,1,0:T(8,128)(2,1)S(1)} %branch_0_fun.13.refs_0_, bf16[3,256,256]{2,1,0:T(8,128)(2,1)S(1)} %collective-permute-done.8.refs_1_.refs_3_.refs_0_, ...), custom_call_target="tpu_custom_call", output_to_operand_aliasing={{}: (9, {})} | custom-call | flops 33554432 | bytes 131072 | tf_op jit(solution)/shard_map/cond/branch_0_fun/pallas_call | solution.py:467
  76.5 6.0 %branch_0_fun.25 = bf16[2048,2048]{1,0:T(8,128)(2,1)} custom-call(s32[18]{0:T(128)S(1)} %pad_add_fusion.place, s32[8,16]{1,0:T(8,128)S(1)} %copy-done.3, bf16[8,2048,256]{2,1,0:T(8,128)(2,1)S(1)} %branch_0_fun.13.refs_0_, bf16[3,256,256]{2,1,0:T(8,128)(2,1)S(1)} %collective-permute-done.11.refs_3_.refs_1_, ...), custom_call_target="tpu_custom_call" | custom-call | flops 33554432 | bytes 131072 | tf_op jit(solution)/shard_map/cond/branch_0_fun/pallas_call | solution.py:467
  (32 shorter events, 6.6 us)
Async XLA Ops:
  2.7 10.1 %collective-permute-start = (bf16[2048,1024]{1,0:T(8,128)(2,1)}, bf16[2048,1024]{1,0:T(8,128)(2,1)}, u32[]{:S(2)}, u32[]{:S(2)}) collective-permute-start(bf16[2048,1024]{1,0:T(8,128)(2,1)} %get-tuple-element.60.own_ref), channel_id=1, source_target_pairs={{0,1},{1,0},{2,3},{3,2},{4,5},{5,4},{6,7},{7,6},{8,9},{9,8},{10,11... | collective-permute-start | bytes 12582920 | tf_op jit(solution)/shard_map/cond/branch_0_fun/ppermute | solution.py:547
  3.2 15.2 %collective-permute-start.1 = (bf16[3,256,256]{2,1,0:T(8,128)(2,1)S(1)}, bf16[3,256,256]{2,1,0:T(8,128)(2,1)S(1)}, u32[]{:S(2)}, u32[]{:S(2)}) collective-permute-start(bf16[3,256,256]{2,1,0:T(8,128)(2,1)S(1)} %get-tuple-element.62), channel_id=1, source_target_pairs={{0,4},{4,8},{8,12},{12,14},{14,10},{10,6},{6,2},{2,0},{1,5},{5,9},... | collective-permute-start | bytes 1179656 | tf_op jit(solution)/shard_map/cond/branch_0_fun/ppermute | solution.py:545
  5.8 12.5 %collective-permute-start.3 = (bf16[3,256,256]{2,1,0:T(8,128)(2,1)S(1)}, bf16[3,256,256]{2,1,0:T(8,128)(2,1)S(1)}, u32[]{:S(2)}, u32[]{:S(2)}) collective-permute-start(bf16[3,256,256]{2,1,0:T(8,128)(2,1)S(1)} %get-tuple-element.65), channel_id=1, source_target_pairs={{4,0},{8,4},{12,8},{14,12},{10,14},{6,10},{2,6},{0,2},{5,1},{9,5},... | collective-permute-start | bytes 1179656 | tf_op jit(solution)/shard_map/cond/branch_0_fun/ppermute | solution.py:545
  9.0 15.2 %collective-permute-start.2 = (bf16[3,256,256]{2,1,0:T(8,128)(2,1)}, bf16[3,256,256]{2,1,0:T(8,128)(2,1)S(1)}, u32[]{:S(2)}, u32[]{:S(2)}) collective-permute-start(bf16[3,256,256]{2,1,0:T(8,128)(2,1)} %get-tuple-element.64), channel_id=1, source_target_pairs={{0,4},{4,8},{8,12},{12,14},{14,10},{10,6},{6,2},{2,0},{1,5},{5,9},... | collective-permute-start | bytes 1179656 | tf_op jit(solution)/shard_map/cond/branch_0_fun/ppermute | solution.py:545
  11.0 15.2 %collective-permute-start.4 = (bf16[3,256,256]{2,1,0:T(8,128)(2,1)}, bf16[3,256,256]{2,1,0:T(8,128)(2,1)S(1)}, u32[]{:S(2)}, u32[]{:S(2)}) collective-permute-start(bf16[3,256,256]{2,1,0:T(8,128)(2,1)} %get-tuple-element.66), channel_id=1, source_target_pairs={{4,0},{8,4},{12,8},{14,12},{10,14},{6,10},{2,6},{0,2},{5,1},{9,5},... | collective-permute-start | bytes 1179656 | tf_op jit(solution)/shard_map/cond/branch_0_fun/ppermute | solution.py:545
  12.7 16.2 %copy-start = (bf16[256,2048]{1,0:T(8,128)(2,1)S(1)}, bf16[256,2048]{1,0:T(8,128)(2,1)}, u32[]{:S(2)}) copy-start(bf16[256,2048]{1,0:T(8,128)(2,1)} %get-tuple-element.63.b_ref.refs_1_) | copy-start | bytes 3145732 | tf_op jit(solution)/shard_map/cond
  12.7 16.2 %copy-start.3 = (s32[8,16]{1,0:T(8,128)S(1)}, s32[8,16]{1,0:T(8,128)}, u32[]{:S(2)}) copy-start(s32[8,16]{1,0:T(8,128)} %get-tuple-element.58.b_mask) | copy-start | bytes 1540 | tf_op jit(solution)/shard_map/cond
  19.0 16.2 %collective-permute-start.6 = (bf16[3,256,256]{2,1,0:T(8,128)(2,1)S(1)}, bf16[3,256,256]{2,1,0:T(8,128)(2,1)S(1)}, u32[]{:S(2)}, u32[]{:S(2)}) collective-permute-start(bf16[3,256,256]{2,1,0:T(8,128)(2,1)S(1)} %get-tuple-element.74), channel_id=1, source_target_pairs={{0,4},{4,8},{8,12},{12,14},{14,10},{10,6},{6,2},{2,0},{1,5},{5,9},... | collective-permute-start | bytes 1179656 | tf_op jit(solution)/shard_map/cond/branch_0_fun/ppermute | solution.py:545
  21.0 14.2 %collective-permute-start.7 = (bf16[3,256,256]{2,1,0:T(8,128)(2,1)S(1)}, bf16[3,256,256]{2,1,0:T(8,128)(2,1)S(1)}, u32[]{:S(2)}, u32[]{:S(2)}) collective-permute-start(bf16[3,256,256]{2,1,0:T(8,128)(2,1)S(1)} %get-tuple-element.75), channel_id=1, source_target_pairs={{4,0},{8,4},{12,8},{14,12},{10,14},{6,10},{2,6},{0,2},{5,1},{9,5},... | collective-permute-start | bytes 1179656 | tf_op jit(solution)/shard_map/cond/branch_0_fun/ppermute | solution.py:545
  26.9 18.8 %collective-permute-start.5 = (bf16[3,256,256]{2,1,0:T(8,128)(2,1)S(1)}, bf16[3,256,256]{2,1,0:T(8,128)(2,1)S(1)}, u32[]{:S(2)}, u32[]{:S(2)}) collective-permute-start(bf16[3,256,256]{2,1,0:T(8,128)(2,1)S(1)} %get-tuple-element.67), channel_id=1, source_target_pairs={{0,4},{4,8},{8,12},{12,14},{14,10},{10,6},{6,2},{2,0},{1,5},{5,9},... | collective-permute-start | bytes 1179656 | tf_op jit(solution)/shard_map/cond/branch_0_fun/ppermute | solution.py:545
  28.5 17.2 %collective-permute-start.9 = (bf16[3,256,256]{2,1,0:T(8,128)(2,1)S(1)}, bf16[3,256,256]{2,1,0:T(8,128)(2,1)S(1)}, u32[]{:S(2)}, u32[]{:S(2)}) collective-permute-start(bf16[3,256,256]{2,1,0:T(8,128)(2,1)S(1)} %get-tuple-element.82), channel_id=1, source_target_pairs={{4,0},{8,4},{12,8},{14,12},{10,14},{6,10},{2,6},{0,2},{5,1},{9,5},... | collective-permute-start | bytes 1179656 | tf_op jit(solution)/shard_map/cond/branch_0_fun/ppermute | solution.py:545
  35.9 15.6 %collective-permute-start.10 = (bf16[3,256,256]{2,1,0:T(8,128)(2,1)S(1)}, bf16[3,256,256]{2,1,0:T(8,128)(2,1)S(1)}, u32[]{:S(2)}, u32[]{:S(2)}) collective-permute-start(bf16[3,256,256]{2,1,0:T(8,128)(2,1)S(1)} %get-tuple-element.83), channel_id=1, source_target_pairs={{4,0},{8,4},{12,8},{14,12},{10,14},{6,10},{2,6},{0,2},{5,1},{9,5},... | collective-permute-start | bytes 1179656 | tf_op jit(solution)/shard_map/cond/branch_0_fun/ppermute | solution.py:545
  35.9 15.6 %collective-permute-start.8 = (bf16[3,256,256]{2,1,0:T(8,128)(2,1)S(1)}, bf16[3,256,256]{2,1,0:T(8,128)(2,1)S(1)}, u32[]{:S(2)}, u32[]{:S(2)}) collective-permute-start(bf16[3,256,256]{2,1,0:T(8,128)(2,1)S(1)} %get-tuple-element.81), channel_id=1, source_target_pairs={{0,4},{4,8},{8,12},{12,14},{14,10},{10,6},{6,2},{2,0},{1,5},{5,9},... | collective-permute-start | bytes 1179656 | tf_op jit(solution)/shard_map/cond/branch_0_fun/ppermute | solution.py:545
  46.4 15.7 %collective-permute-start.12 = (bf16[3,256,256]{2,1,0:T(8,128)(2,1)S(1)}, bf16[3,256,256]{2,1,0:T(8,128)(2,1)S(1)}, u32[]{:S(2)}, u32[]{:S(2)}) collective-permute-start(bf16[3,256,256]{2,1,0:T(8,128)(2,1)S(1)} %get-tuple-element.89), channel_id=1, source_target_pairs={{0,4},{4,8},{8,12},{12,14},{14,10},{10,6},{6,2},{2,0},{1,5},{5,9},... | collective-permute-start | bytes 1179656 | tf_op jit(solution)/shard_map/cond/branch_0_fun/ppermute | solution.py:545
  48.0 14.1 %collective-permute-start.13 = (bf16[3,256,256]{2,1,0:T(8,128)(2,1)S(1)}, bf16[3,256,256]{2,1,0:T(8,128)(2,1)S(1)}, u32[]{:S(2)}, u32[]{:S(2)}) collective-permute-start(bf16[3,256,256]{2,1,0:T(8,128)(2,1)S(1)} %get-tuple-element.90), channel_id=1, source_target_pairs={{4,0},{8,4},{12,8},{14,12},{10,14},{6,10},{2,6},{0,2},{5,1},{9,5},... | collective-permute-start | bytes 1179656 | tf_op jit(solution)/shard_map/cond/branch_0_fun/ppermute | solution.py:545
  52.1 14.8 %collective-permute-start.11 = (bf16[3,256,256]{2,1,0:T(8,128)(2,1)S(1)}, bf16[3,256,256]{2,1,0:T(8,128)(2,1)S(1)}, u32[]{:S(2)}, u32[]{:S(2)}) collective-permute-start(bf16[3,256,256]{2,1,0:T(8,128)(2,1)S(1)} %get-tuple-element.84), channel_id=1, source_target_pairs={{0,4},{4,8},{8,12},{12,14},{14,10},{10,6},{6,2},{2,0},{1,5},{5,9},... | collective-permute-start | bytes 1179656 | tf_op jit(solution)/shard_map/cond/branch_0_fun/ppermute | solution.py:545
  53.8 14.7 %collective-permute-start.15 = (bf16[3,256,256]{2,1,0:T(8,128)(2,1)S(1)}, bf16[3,256,256]{2,1,0:T(8,128)(2,1)S(1)}, u32[]{:S(2)}, u32[]{:S(2)}) collective-permute-start(bf16[3,256,256]{2,1,0:T(8,128)(2,1)S(1)} %get-tuple-element.96), channel_id=1, source_target_pairs={{4,0},{8,4},{12,8},{14,12},{10,14},{6,10},{2,6},{0,2},{5,1},{9,5},... | collective-permute-start | bytes 1179656 | tf_op jit(solution)/shard_map/cond/branch_0_fun/ppermute | solution.py:545
  62.7 13.8 %collective-permute-start.14 = (bf16[3,256,256]{2,1,0:T(8,128)(2,1)S(1)}, bf16[3,256,256]{2,1,0:T(8,128)(2,1)S(1)}, u32[]{:S(2)}, u32[]{:S(2)}) collective-permute-start(bf16[3,256,256]{2,1,0:T(8,128)(2,1)S(1)} %get-tuple-element.95), channel_id=1, source_target_pairs={{0,4},{4,8},{8,12},{12,14},{14,10},{10,6},{6,2},{2,0},{1,5},{5,9},... | collective-permute-start | bytes 1179656 | tf_op jit(solution)/shard_map/cond/branch_0_fun/ppermute | solution.py:545
  64.4 12.2 %collective-permute-start.16 = (bf16[3,256,256]{2,1,0:T(8,128)(2,1)S(1)}, bf16[3,256,256]{2,1,0:T(8,128)(2,1)S(1)}, u32[]{:S(2)}, u32[]{:S(2)}) collective-permute-start(bf16[3,256,256]{2,1,0:T(8,128)(2,1)S(1)} %get-tuple-element.97), channel_id=1, source_target_pairs={{4,0},{8,4},{12,8},{14,12},{10,14},{6,10},{2,6},{0,2},{5,1},{9,5},... | collective-permute-start | bytes 1179656 | tf_op jit(solution)/shard_map/cond/branch_0_fun/ppermute | solution.py:545
